TPU v7x, 128 devices: a whole 4x4x4 slice. The times are simulated.
128 devices in a mesh: deme: 16 (over y, z), gen: 8 (over x, core).
Axes of the slice: x: 4, y: 4, z: 4, core: 2. Of those that a mesh axis runs over, the one named last changes fastest.
Arguments:
- freqs: float32 [4096, 256, 512], P('deme', 'gen'), may hold values from 0 to 1
- start_basis: float32 [512, 128], replicated, may hold values from -0.25 to 0.25
Outputs:
- core: float32 [4096, 256, 128], P('deme', 'gen')
- factor: float32 [512, 128], replicated
All inputs are finite; a program needn't handle non-finite values.
Results may differ from a plain program's by a relative error of at most 0.0003.
Values sent between devices are 32-bit elements; how exact they have to be, the bound alone decides.
No kernel may reach another device: no remote copies, remote signals or barrier semaphores. Data moves between devices by JAX's collectives and lax.ppermute only.
A program may use at most 64 MiB of HBM per device.

v0:
```python
import jax
import jax.numpy as jnp
from jax import lax
from jax.sharding import PartitionSpec as P

ITERS = 4


def orthonormal(z):
    small = jnp.dot(z.T, z, precision=lax.Precision.HIGHEST, preferred_element_type=jnp.float32)
    lower = jnp.linalg.cholesky(small)
    return jax.scipy.linalg.solve_triangular(lower, z.T, lower=True).T


def times_basis(matrix, basis):
    return jnp.dot(
        matrix, basis, precision=lax.Precision.HIGHEST, preferred_element_type=jnp.float32
    )


def local(freqs, start_basis):
    deme_count, gen_count, loci = freqs.shape
    demes_all = deme_count * lax.axis_size("deme")
    totals = lax.psum(jnp.sum(freqs, axis=0), "deme")
    centered = (freqs - totals / demes_all).reshape(deme_count * gen_count, loci)
    scale = 1.0 / (demes_all * gen_count * lax.axis_size("gen"))
    basis = start_basis
    gram = (
        lax.psum(
            lax.dot_general(
                centered,
                centered,
                (((0,), (0,)), ((), ())),
                precision=lax.Precision.HIGHEST,
                preferred_element_type=jnp.float32,
            ),
            ("deme", "gen"),
        )
        * scale
    )
    for step in range(ITERS):
        basis = orthonormal(times_basis(gram, basis))
    core = jnp.dot(
        centered, basis, precision=lax.Precision.HIGHEST, preferred_element_type=jnp.float32
    )
    return (core.reshape(deme_count, gen_count, basis.shape[1]), basis)


def solution(mesh):
    in_specs = (P("deme", "gen", None), P())
    out_specs = (P("deme", "gen", None), P())
    return jax.shard_map(local, mesh=mesh, in_specs=in_specs, out_specs=out_specs, check_vma=False)
```

profile of v0, /device:TPU:1, one launch (start us, length us, event | category | flops | bytes accessed | tf_op | source)
XLA Modules:
  0.0 410.2 jit_solution(4716284155882600036)
XLA Ops:
  7.2 7.5 %reduce_sum.9 = f32[32,512]{1,0:T(8,128)} reduce(f32[256,32,512]{2,1,0:T(8,128)} %param.5, f32[]{:T(128)} %constant.35.clone.1), dimensions={0}, to_apply=%region_0.0 | reduce | flops 4177920 | bytes 16842756 | tf_op jit(solution)/shard_map/reduce_sum | solution.py:24
  14.8 82.8 %all-reduce.3.cloned.1.call-done = f32[32,512]{1,0:T(8,128)} async-done(((f32[32,512]{1,0:T(8,128)}), f32[32,512]{1,0:T(8,128)}) %all-reduce.3.cloned.1.call-update) | async-done | bytes 65552 | tf_op jit(solution)/shard_map/psum | solution.py:24
  97.5 0.8 broadcast_multiply_fusion
  98.4 32.5 %fusion.6 = f32[512,512]{1,0:T(8,128)} fusion(f32[256,32,512]{2,1,0:T(8,128)} %param.5, f32[32,512]{1,0:T(8,128)S(1)} %broadcast_multiply_fusion), kind=kOutput, calls=%fused_computation.6 | convolution fusion | flops 25773998080 | bytes 17891328 | tf_op jit(solution)/shard_map/dot_general | solution.py:30
  130.9 148.3 %all-reduce.5.cloned.1.call-done = f32[512,512]{1,0:T(8,128)} async-done(((f32[512,512]{1,0:T(8,128)}), f32[512,512]{1,0:T(8,128)}) %all-reduce.5.cloned.1.call-update) | async-done | bytes 1048592 | tf_op jit(solution)/shard_map/psum | solution.py:29
  279.2 2.2 fusion.15
  282.1 11.7 %cholesky.74 = f32[128,128]{1,0:T(8,128)S(1)} custom-call(f32[128,128]{1,0:T(8,128)S(1)} %fusion.41), custom_call_target="Cholesky" | custom-call | tf_op jit(solution)/shard_map/jit(cholesky)/cholesky | solution.py:11
  293.9 0.6 compare_reduce_fusion.3
  294.5 0.7 fusion.30
  295.2 9.8 %custom-call.8 = f32[1,128,128]{1,2,0:T(8,128)S(1)} custom-call(f32[1,128,128]{2,1,0:T(8,128)S(1)} %fusion.30), custom_call_target="InvertDiagBlocksLowerTriangular" | custom-call | tf_op jit(solution)/shard_map/jit(_solve_triangular)/triangular_solve | solution.py:12
  305.4 2.2 fusion.13
  308.3 11.9 %cholesky.85 = f32[128,128]{1,0:T(8,128)S(1)} custom-call(f32[128,128]{1,0:T(8,128)S(1)} %fusion.39), custom_call_target="Cholesky" | custom-call | tf_op jit(solution)/shard_map/jit(cholesky)/cholesky | solution.py:11
  320.9 0.7 fusion.31
  321.6 9.8 %custom-call.9 = f32[1,128,128]{1,2,0:T(8,128)S(1)} custom-call(f32[1,128,128]{2,1,0:T(8,128)S(1)} %fusion.31), custom_call_target="InvertDiagBlocksLowerTriangular" | custom-call | tf_op jit(solution)/shard_map/jit(_solve_triangular)/triangular_solve | solution.py:12
  331.8 2.2 fusion.11
  334.7 11.7 %cholesky.96 = f32[128,128]{1,0:T(8,128)S(1)} custom-call(f32[128,128]{1,0:T(8,128)S(1)} %fusion.37), custom_call_target="Cholesky" | custom-call | tf_op jit(solution)/shard_map/jit(cholesky)/cholesky | solution.py:11
  347.1 0.7 fusion.32
  347.8 9.8 %custom-call.10 = f32[1,128,128]{1,2,0:T(8,128)S(1)} custom-call(f32[1,128,128]{2,1,0:T(8,128)S(1)} %fusion.32), custom_call_target="InvertDiagBlocksLowerTriangular" | custom-call | tf_op jit(solution)/shard_map/jit(_solve_triangular)/triangular_solve | solution.py:12
  358.0 2.6 fusion.9
  361.3 11.7 %cholesky.107 = f32[128,128]{1,0:T(8,128)S(1)} custom-call(f32[128,128]{1,0:T(8,128)S(1)} %fusion.35), custom_call_target="Cholesky" | custom-call | tf_op jit(solution)/shard_map/jit(cholesky)/cholesky | solution.py:11
  373.7 0.7 fusion.33
  374.4 9.8 %custom-call.11 = f32[1,128,128]{1,2,0:T(8,128)S(1)} custom-call(f32[1,128,128]{2,1,0:T(8,128)S(1)} %fusion.33), custom_call_target="InvertDiagBlocksLowerTriangular" | custom-call | tf_op jit(solution)/shard_map/jit(_solve_triangular)/triangular_solve | solution.py:12
  384.6 17.7 %fusion = f32[256,32,128]{2,1,0:T(8,128)} fusion(f32[256,32,512]{2,1,0:T(8,128)} %param.5, f32[32,512]{1,0:T(8,128)S(1)} %broadcast_multiply_fusion, f32[128,512]{1,0:T(8,128)S(1)} %fusion.22), kind=kOutput, calls=%fused_computation | convolution fusion | flops 6446645248 | bytes 21299200 | tf_op jit(solution)/shard_map/dot_general | solution.py:43
  402.3 0.8 copy.12
  (29 shorter events, 6.6 us)
Async XLA Ops:
  7.2 272.0 %copy-start = (f32[512,128]{1,0:T(8,128)S(1)}, f32[512,128]{1,0:T(8,128)}, u32[]{:S(2)}) copy-start(f32[512,128]{1,0:T(8,128)} %param.6) | copy-start | bytes 786436
  7.2 90.4 %all-reduce.3.cloned.1.call-start = ((), (), s32[]{:S(2)}) async-start(), calls=%async_computation | async-start | bytes 131072 | tf_op jit(solution)/shard_map/psum | solution.py:24
  14.7 264.5 %all-reduce.5.cloned.1.call-start = ((), (), s32[]{:S(2)}) async-start(), calls=%async_computation.1 | async-start | bytes 2097152 | tf_op jit(solution)/shard_map/psum | solution.py:29
Sparse Core Ops, SparseCore 0:
  14.8 82.6 all-reduce.2
  131.0 148.1 all-reduce.4
where the time goes:
time: 417 us; the launch traced here: 410 us
  waiting for transfers between devices  231 us (55%)
  other arithmetic  100 us (24%)
  matrix products  63.4 us (15%)
  between operations  14.4 us (3%)
    psum x1, waiting for transfers between devices, local(): lax.psum(lax.dot_general(centered, centered, (((0,), (0,)), ((), ())), pr...  148 us
    psum x1, waiting for transfers between devices, local(): totals = lax.psum(jnp.sum(freqs, axis=0), 'deme')  82.8 us
    another operation x12, other arithmetic, orthonormal(): lower = jnp.linalg.cholesky(small)  49.7 us
    another operation x8, other arithmetic, orthonormal(): return jax.scipy.linalg.solve_triangular(lower, z.T, lower=True).T  41.9 us
    dot_general x1, matrix products, local(): lax.dot_general(centered, centered, (((0,), (0,)), ((), ())), precision=l...  32.5 us
    dot_general x1, matrix products, local(): jnp.dot(centered, basis, precision=lax.Precision.HIGHEST, preferred_eleme...  17.7 us
    dot_general x4, matrix products, times_basis(): jnp.dot(matrix, basis, precision=lax.Precision.HIGHEST, preferred_element...  9.24 us
  transfers between devices with their start and end apart: 2, of which 2 were waited for; matrix products, arithmetic and copies ran while one was open for 0% of the time, Pallas kernels for 0%

commit v1 on v0

v1 whole, which is shorter than its diff:
```python
import jax
import jax.numpy as jnp
from jax import lax
from jax.experimental import pallas as pl
from jax.experimental.pallas import tpu as pltpu
from jax.sharding import PartitionSpec as P

ITERS = 4
LOCI = 512
RANK = 128
BLOCK = 128
PIECE = 80
PACKED = 1280
PAIRS = [(i, j) for i in range(4) for j in range(i, 4)]
DEMES = 256
GENS = 32
CHUNK = 32
MEAN_ROWS = 128
AXES = ("deme", "gen")
MIB = 1024 * 1024


def place():
    deme, gen = lax.axis_index("deme"), lax.axis_index("gen")
    y, z, core = deme // 4, deme % 4, gen % 2
    return jnp.where(core == 0, z, y), jnp.where(core == 0, y, z), core


def piece_row(core, first, second):
    return PIECE * jnp.where(core == 0, 4 * first + second, 4 * second + first)


def shifted(kind, k):
    pairs = []
    for device in range(128):
        deme, gen = divmod(device, 8)
        y, z = divmod(deme, 4)
        x, core = divmod(gen, 2)
        if kind == "x":
            x = (x + k) % 4
        elif kind == "core":
            core = 1 - core
        elif (kind == "first") == (core == 0):
            z = (z + k) % 4
        else:
            y = (y + k) % 4
        pairs.append((device, (4 * y + z) * 8 + 2 * x + core))
    return pairs


def send(value, kind, k):
    return lax.ppermute(value, AXES, shifted(kind, k))


def cross(a, b, precision=None):
    return lax.dot_general(
        a, b, (((0,), (0,)), ((), ())), precision=precision, preferred_element_type=jnp.float32
    )


def gram_kernel(x_ref, *refs):
    outs, (split, top, low, shift, total, packed) = refs[:4], refs[4:]
    step = pl.program_id(0)

    @pl.when(step == 0)
    def _():
        shift[...] = jnp.sum(x_ref[...], axis=0) * (1.0 / CHUNK)
        total[...] = jnp.zeros_like(total)
        top[...] = jnp.zeros_like(top)
        low[...] = jnp.zeros_like(low)

    d = x_ref[...] - shift[...][None]
    total[...] += jnp.sum(d, axis=0)
    d = d.reshape(CHUNK * GENS, LOCI)
    hi = d.astype(jnp.bfloat16)
    split[:, :LOCI] = hi
    split[:, LOCI:] = (d - hi.astype(jnp.float32)).astype(jnp.bfloat16)
    top[...] += cross(split[:, :256], split[...])
    low[...] += cross(split[:, 256:512], split[:, 256:])

    @pl.when(step == pl.num_programs(0) - 1)
    def _():
        sums = total[...]
        offset = cross(sums, sums, lax.Precision.HIGHEST) * (1.0 / DEMES)

        def high(i, j):
            if i < 2:
                return top[BLOCK * i : BLOCK * (i + 1), BLOCK * j : BLOCK * (j + 1)]
            return low[BLOCK * (i - 2) : BLOCK * (i - 1), BLOCK * (j - 2) : BLOCK * (j - 1)]

        def mixed(i, j):
            if i < 2:
                return top[BLOCK * i : BLOCK * (i + 1), LOCI + BLOCK * j : LOCI + BLOCK * (j + 1)]
            return low[BLOCK * (i - 2) : BLOCK * (i - 1), 256 + BLOCK * j : 256 + BLOCK * (j + 1)]

        for n, (i, j) in enumerate(PAIRS):
            block = high(i, j) + (mixed(i, j) + mixed(j, i).T)
            packed[BLOCK * n : BLOCK * (n + 1), :] = (
                block - offset[BLOCK * i : BLOCK * (i + 1), BLOCK * j : BLOCK * (j + 1)]
            )
        mean = shift[...] + sums * (1.0 / DEMES)
        first, second, core = place()
        for k, out in enumerate(outs):
            to = (first + k) % 4
            for j in range(4):
                row = pl.multiple_of(piece_row(core, to, j), 8)
                out[PIECE * j : PIECE * (j + 1), :] = packed[pl.ds(row, PIECE), :]
                out[4 * PIECE + 32 * j : 4 * PIECE + 32 * (j + 1), :] = mean[:, BLOCK * j : BLOCK * (j + 1)]


def local_gram(freqs):
    rows = 4 * PIECE + MEAN_ROWS
    return pl.pallas_call(
        gram_kernel,
        grid=(DEMES // CHUNK,),
        in_specs=[pl.BlockSpec((CHUNK, GENS, LOCI), lambda t: (t, 0, 0))],
        out_specs=[pl.BlockSpec((rows, BLOCK), lambda t: (0, 0))] * 4,
        out_shape=[jax.ShapeDtypeStruct((rows, BLOCK), jnp.float32)] * 4,
        scratch_shapes=[
            pltpu.VMEM((CHUNK * GENS, 2 * LOCI), jnp.bfloat16),
            pltpu.VMEM((256, 1024), jnp.float32),
            pltpu.VMEM((256, 768), jnp.float32),
            pltpu.VMEM((GENS, LOCI), jnp.float32),
            pltpu.VMEM((GENS, LOCI), jnp.float32),
            pltpu.VMEM((PACKED, BLOCK), jnp.float32),
        ],
        compiler_params=pltpu.CompilerParams(vmem_limit_bytes=40 * MIB),
        cost_estimate=pl.CostEstimate(flops=2 * 8192 * 512 * 900, bytes_accessed=20 * MIB, transcendentals=0),
        name="local_gram",
    )(freqs)


def merge(refs, rows, weight, packed):
    wide = [
        jnp.concatenate([ref[rows + 32 * j : rows + 32 * (j + 1), :] for j in range(4)], axis=1) for ref in refs
    ]
    mean = ((wide[0] + wide[2]) + (wide[1] + wide[3])) * 0.25
    delta = jnp.concatenate([part - mean for part in wide], axis=0)
    for i in range(4):
        product = cross(delta[:, BLOCK * i : BLOCK * (i + 1)], delta[:, BLOCK * i :], lax.Precision.HIGHEST)
        for j in range(i, 4):
            n = PAIRS.index((i, j))
            packed[BLOCK * n : BLOCK * (n + 1), :] = product[:, BLOCK * (j - i) : BLOCK * (j - i + 1)] * weight
    return mean


def first_kernel(*refs):
    ins, outs, (packed, summed) = refs[:4], refs[4:8], refs[8:]
    mean = merge(ins, 4 * PIECE, float(DEMES), packed)
    first, second, core = place()
    for j in range(4):
        rows = slice(PIECE * j, PIECE * (j + 1))
        row = pl.multiple_of(piece_row(core, first, j), 8)
        summed[rows, :] = ((ins[0][rows, :] + ins[2][rows, :]) + (ins[1][rows, :] + ins[3][rows, :])) + packed[
            pl.ds(row, PIECE), :
        ]
    for k, out in enumerate(outs):
        row = pl.multiple_of(PIECE * ((second + k) % 4), 8)
        out[:PIECE, :] = summed[pl.ds(row, PIECE), :]
        for j in range(4):
            out[PIECE + 32 * j : PIECE + 32 * (j + 1), :] = mean[:, BLOCK * j : BLOCK * (j + 1)]


def second_kernel(*refs):
    ins, (out, mean_out), (packed,) = refs[:4], refs[4:6], refs[6:]
    mean_out[...] = merge(ins, PIECE, 4.0 * DEMES, packed)
    first, second, core = place()
    row = pl.multiple_of(piece_row(core, first, second), 8)
    rows = slice(0, PIECE)
    out[...] = ((ins[0][rows, :] + ins[2][rows, :]) + (ins[1][rows, :] + ins[3][rows, :])) + packed[
        pl.ds(row, PIECE), :
    ]


def merge_first(parts):
    rows = PIECE + MEAN_ROWS
    return pl.pallas_call(
        first_kernel,
        out_shape=[jax.ShapeDtypeStruct((rows, BLOCK), jnp.float32)] * 4,
        scratch_shapes=[pltpu.VMEM((PACKED, BLOCK), jnp.float32), pltpu.VMEM((4 * PIECE, BLOCK), jnp.float32)],
        compiler_params=pltpu.CompilerParams(vmem_limit_bytes=16 * MIB),
        name="merge_first",
    )(*parts)


def merge_second(parts):
    return pl.pallas_call(
        second_kernel,
        out_shape=[
            jax.ShapeDtypeStruct((PIECE, BLOCK), jnp.float32),
            jax.ShapeDtypeStruct((GENS, LOCI), jnp.float32),
        ],
        scratch_shapes=[pltpu.VMEM((PACKED, BLOCK), jnp.float32)],
        compiler_params=pltpu.CompilerParams(vmem_limit_bytes=16 * MIB),
        name="merge_second",
    )(*parts)


def inverse_cholesky(s):
    full = (8, RANK)
    lane = lax.broadcasted_iota(jnp.int32, full, 1)
    sub = lax.broadcasted_iota(jnp.int32, full, 0)
    count = RANK // 8
    rows = [s[8 * i : 8 * i + 8, :] for i in range(count)]
    for k in range(count):
        cols = {
            i: [jnp.broadcast_to(rows[i][:, 8 * k + j : 8 * k + j + 1], full) for j in range(8)]
            for i in range(k, count)
        }
        inverses = []
        for j in range(8):
            pivot = cols[k][j]
            inverse = 1.0 / jnp.broadcast_to(pivot[j : j + 1, :], full)
            inverses.append(inverse)
            for l in range(j + 1, 8):
                ratio = jnp.broadcast_to(pivot[l : l + 1, :], full) * inverse
                for i in range(k, count):
                    cols[i][l] = cols[i][l] - cols[i][j] * ratio
        here = (lane >= 8 * k) & (lane < 8 * k + 8)
        own = jnp.where(here, jnp.where(lane - 8 * k == sub, 1.0, 0.0), rows[k])
        scaled = []
        scale = inverses[0]
        for j in range(8):
            scaled.append(jnp.broadcast_to(own[j : j + 1, :], full) * inverses[j])
            if j < 7:
                own = own - jnp.where(sub > j, cols[k][j], 0.0) * scaled[j]
            if j:
                scale = jnp.where(sub == j, inverses[j], scale)
        for i in range(k + 1, count):
            rest = jnp.where(here, 0.0, rows[i])
            for j in range(8):
                rest = rest - cols[i][j] * scaled[j]
            rows[i] = rest
        rows[k] = jnp.where(lane <= 8 * k + sub, own * jnp.sqrt(scale), 0.0)
    return jnp.concatenate(rows, axis=0)


STEP = 16
STEPS = DEMES // STEP
LOADS = 4


def core_kernel(p0, p1, p2, p3, start_ref, mean_ref, x_hbm, core_hbm, factor_ref, x, core, packed, gram, loads, stores):
    def load(n):
        part = pl.ds(n * (DEMES // LOADS), DEMES // LOADS)
        return pltpu.make_async_copy(x_hbm.at[part], x.at[part], loads.at[n])

    def store(n):
        part = pl.ds(n * STEP, STEP)
        return pltpu.make_async_copy(core.at[part], core_hbm.at[part], stores.at[n])

    for n in range(LOADS):
        load(n).start()

    first, second, core_id = place()
    for k, part in enumerate((p0, p1, p2, p3)):
        for l in range(4):
            row = pl.multiple_of(piece_row(core_id, (first + 4 - k) % 4, (second + 4 - l) % 4), 8)
            packed[pl.ds(row, PIECE), :] = part[PIECE * l : PIECE * (l + 1), :]
    for n, (i, j) in enumerate(PAIRS):
        block = packed[BLOCK * n : BLOCK * (n + 1), :] * (1.0 / (4096 * 256))
        gram[BLOCK * i : BLOCK * (i + 1), BLOCK * j : BLOCK * (j + 1)] = block
        if i != j:
            gram[BLOCK * j : BLOCK * (j + 1), BLOCK * i : BLOCK * (i + 1)] = block.T

    def body(_, basis):
        z = jnp.dot(basis, gram[...], precision=lax.Precision.HIGHEST, preferred_element_type=jnp.float32)
        small = lax.dot_general(
            z, z, (((1,), (1,)), ((), ())), precision=lax.Precision.HIGHEST, preferred_element_type=jnp.float32
        )
        return jnp.dot(
            inverse_cholesky(small), z, precision=lax.Precision.HIGHEST, preferred_element_type=jnp.float32
        )

    basis = lax.fori_loop(0, ITERS, body, start_ref[...].T)
    factor = basis.T
    factor_ref[...] = factor
    hi = factor.astype(jnp.bfloat16)
    lo = (factor - hi.astype(jnp.float32)).astype(jnp.bfloat16)
    both = jnp.concatenate([hi, lo], axis=1)
    mean = mean_ref[...]
    for n in range(LOADS):
        load(n).wait()

    def step(n, carry):
        part = pl.ds(n * STEP, STEP)
        d = (x[part] - mean[None]).reshape(STEP * GENS, LOCI)
        d_hi = d.astype(jnp.bfloat16)
        d_lo = (d - d_hi.astype(jnp.float32)).astype(jnp.bfloat16)
        wide = jnp.dot(d_hi, both, preferred_element_type=jnp.float32)
        rest = jnp.dot(d_lo, hi, preferred_element_type=jnp.float32)
        core[part] = (wide[:, :RANK] + (wide[:, RANK:] + rest)).reshape(STEP, GENS, RANK)
        store(n).start()
        return carry

    lax.fori_loop(0, STEPS, step, 0)
    for n in range(STEPS):
        store(n).wait()


def iterate(parts, start_basis, mean, freqs):
    vmem = pl.BlockSpec(memory_space=pltpu.VMEM)
    hbm = pl.BlockSpec(memory_space=pltpu.HBM)
    return pl.pallas_call(
        core_kernel,
        in_specs=[vmem] * 6 + [hbm],
        out_specs=[hbm, vmem],
        out_shape=[
            jax.ShapeDtypeStruct((DEMES, GENS, RANK), jnp.float32),
            jax.ShapeDtypeStruct((LOCI, RANK), jnp.float32),
        ],
        scratch_shapes=[
            pltpu.VMEM((DEMES, GENS, LOCI), jnp.float32),
            pltpu.VMEM((DEMES, GENS, RANK), jnp.float32),
            pltpu.VMEM((PACKED, BLOCK), jnp.float32),
            pltpu.VMEM((LOCI, LOCI), jnp.float32),
            pltpu.SemaphoreType.DMA((LOADS,)),
            pltpu.SemaphoreType.DMA((STEPS,)),
        ],
        compiler_params=pltpu.CompilerParams(vmem_limit_bytes=48 * MIB),
        name="iterate",
    )(*parts, start_basis, mean, freqs)


def local(freqs, start_basis):
    out = local_gram(freqs)
    parts = merge_first([out[0]] + [send(out[k], "first", k) for k in (1, 2, 3)])
    shard, mean = merge_second([parts[0]] + [send(parts[k], "second", k) for k in (1, 2, 3)])
    one, two, three = [send(shard, "x", k) for k in (1, 2, 3)]
    shard = (shard + two) + (one + three)
    shard = shard + send(shard, "core", 1)
    row = jnp.concatenate([shard] + [send(shard, "second", k) for k in (1, 2, 3)], axis=0)
    rows = [row] + [send(row, "first", k) for k in (1, 2, 3)]
    return tuple(iterate(rows, start_basis, mean, freqs))


def solution(mesh):
    in_specs = (P("deme", "gen", None), P())
    out_specs = (P("deme", "gen", None), P())
    return jax.shard_map(local, mesh=mesh, in_specs=in_specs, out_specs=out_specs, check_vma=False)
```

time: 417 us -> 99.9 us (0.24); the launches traced: 410 us -> 98.1 us
  waiting for transfers between devices: 231 us -> 22.3 us
  other arithmetic: 100 us -> 0.03 us
  matrix products: 63.4 us -> 0 us
  Pallas kernels: 0 us -> 48.1 us
  starting transfers between devices: 0.08 us -> 26.8 us
  between operations: 14.4 us -> 0.85 us
    psum x2 -> x0, waiting for transfers between devices: 231 us -> none  [the longest x1 148 us: local(): lax.psum(lax.dot_general(centered, centered, (((0,), (0,)), ((), ())), pr...]
    another operation x20 -> x0, other arithmetic: 91.6 us -> none  [the longest x12 49.7 us: orthonormal(): lower = jnp.linalg.cholesky(small)]
    dot_general x10 -> x0, matrix products: 61.7 us -> none  [the longest x1 32.5 us: local(): lax.dot_general(centered, centered, (((0,), (0,)), ((), ())), precision=l...]
    pallas_call x0 -> x4, Pallas kernels: none -> 48.1 us  [the longest x1 32.1 us: iterate(): pl.pallas_call(core_kernel, in_specs=[vmem] * 6 + [hbm], out_specs=[hbm,...]
    ppermute x0 -> x16, starting transfers between devices: none -> 26.8 us  [send(): return lax.ppermute(value, AXES, shifted(kind, k))]
    ppermute x0 -> x16, waiting for transfers between devices: none -> 22.3 us  [send(): return lax.ppermute(value, AXES, shifted(kind, k))]
    reduce_sum x1 -> x0, other arithmetic: 7.47 us -> none  [local(): totals = lax.psum(jnp.sum(freqs, axis=0), 'deme')]
  transfers between devices with their start and end apart: 2 -> 16, of which waited for: 2 -> 12; matrix products, arithmetic and copies ran while one was open for 0% -> 0% of each run, Pallas kernels for 0% -> 0%
where the time goes in v1:
time: 99.9 us; the launch traced here: 98.1 us
  Pallas kernels  48.1 us (48%)
  starting transfers between devices  26.8 us (27%)
  waiting for transfers between devices  22.3 us (22%)
    pallas_call x1, Pallas kernels, iterate(): pl.pallas_call(core_kernel, in_specs=[vmem] * 6 + [hbm], out_specs=[hbm,...  32.1 us
    ppermute x16, starting transfers between devices, send(): return lax.ppermute(value, AXES, shifted(kind, k))  26.8 us
    ppermute x16, waiting for transfers between devices, send(): return lax.ppermute(value, AXES, shifted(kind, k))  22.3 us
    pallas_call x1, Pallas kernels, local_gram(): pl.pallas_call(gram_kernel, grid=(DEMES // CHUNK,), in_specs=[pl.BlockSpe...  14.5 us
  transfers between devices with their start and end apart: 16, of which 12 were waited for; matrix products, arithmetic and copies ran while one was open for 0% of the time, Pallas kernels for 0%

profile of v1, /device:TPU:1, one launch (start us, length us, event | category | flops | bytes accessed | tf_op | source)
XLA Modules:
  0.0 98.1 jit_solution(4878549232146910538)
XLA Ops:
  0.6 14.5 %local_gram.1 = (f32[448,128]{1,0:T(8,128)S(1)}, f32[448,128]{1,0:T(8,128)S(1)}, f32[448,128]{1,0:T(8,128)S(1)}, f32[448,128]{1,0:T(8,128)S(1)}) custom-call(f32[256,32,512]{2,1,0:T(8,128)} %x_hbm.1), custom_call_target="tpu_custom_call" | custom-call | flops 7549747200 | bytes 20971520 | tf_op jit(solution)/shard_map/local_gram/pallas_call | solution.py:113
  15.1 2.2 %collective-permute-start = (f32[448,128]{1,0:T(8,128)S(1)}, f32[448,128]{1,0:T(8,128)S(1)}, u32[]{:S(2)}, u32[]{:S(2)}) collective-permute-start(f32[448,128]{1,0:T(8,128)S(1)} %get-tuple-element.13), channel_id=1, source_target_pairs={{0,8},{1,33},{2,10},{3,35},{4,12},{5,37},{6,14},{7,39},{8,16},{9,4... | collective-permute-start | bytes 688136 | tf_op jit(solution)/shard_map/ppermute | solution.py:52
  17.3 2.6 %collective-permute-start.1 = (f32[448,128]{1,0:T(8,128)S(1)}, f32[448,128]{1,0:T(8,128)S(1)}, u32[]{:S(2)}, u32[]{:S(2)}) collective-permute-start(f32[448,128]{1,0:T(8,128)S(1)} %get-tuple-element.14), channel_id=1, source_target_pairs={{0,16},{1,65},{2,18},{3,67},{4,20},{5,69},{6,22},{7,71},{8,24},{9,... | collective-permute-start | bytes 688136 | tf_op jit(solution)/shard_map/ppermute | solution.py:52
  20.0 1.1 %collective-permute-start.2 = (f32[448,128]{1,0:T(8,128)S(1)}, f32[448,128]{1,0:T(8,128)S(1)}, u32[]{:S(2)}, u32[]{:S(2)}) collective-permute-start(f32[448,128]{1,0:T(8,128)S(1)} %get-tuple-element.15), channel_id=1, source_target_pairs={{0,24},{1,97},{2,26},{3,99},{4,28},{5,101},{6,30},{7,103},{8,0},{9... | collective-permute-start | bytes 688136 | tf_op jit(solution)/shard_map/ppermute | solution.py:52
  21.0 1.5 %collective-permute-done.refs_1_ = f32[448,128]{1,0:T(8,128)S(1)} collective-permute-done((f32[448,128]{1,0:T(8,128)S(1)}, f32[448,128]{1,0:T(8,128)S(1)}, u32[]{:S(2)}, u32[]{:S(2)}) %collective-permute-start) | collective-permute-done | bytes 229408 | tf_op jit(solution)/shard_map/ppermute | solution.py:52
  22.5 3.6 %collective-permute-done.1.refs_2_ = f32[448,128]{1,0:T(8,128)S(1)} collective-permute-done((f32[448,128]{1,0:T(8,128)S(1)}, f32[448,128]{1,0:T(8,128)S(1)}, u32[]{:S(2)}, u32[]{:S(2)}) %collective-permute-start.1) | collective-permute-done | bytes 229408 | tf_op jit(solution)/shard_map/ppermute | solution.py:52
  26.1 0.8 merge_first.1
  26.9 1.4 %collective-permute-start.3 = (f32[208,128]{1,0:T(8,128)S(1)}, f32[208,128]{1,0:T(8,128)S(1)}, u32[]{:S(2)}, u32[]{:S(2)}) collective-permute-start(f32[208,128]{1,0:T(8,128)S(1)} %get-tuple-element.17), channel_id=1, source_target_pairs={{0,32},{1,9},{2,34},{3,11},{4,36},{5,13},{6,38},{7,15},{8,40},{9,1... | collective-permute-start | bytes 319496 | tf_op jit(solution)/shard_map/ppermute | solution.py:52
  28.3 3.3 %collective-permute-start.4 = (f32[208,128]{1,0:T(8,128)S(1)}, f32[208,128]{1,0:T(8,128)S(1)}, u32[]{:S(2)}, u32[]{:S(2)}) collective-permute-start(f32[208,128]{1,0:T(8,128)S(1)} %get-tuple-element.18), channel_id=1, source_target_pairs={{0,64},{1,17},{2,66},{3,19},{4,68},{5,21},{6,70},{7,23},{8,72},{9,... | collective-permute-start | bytes 319496 | tf_op jit(solution)/shard_map/ppermute | solution.py:52
  32.5 2.3 %collective-permute-done.4.refs_2_ = f32[208,128]{1,0:T(8,128)S(1)} collective-permute-done((f32[208,128]{1,0:T(8,128)S(1)}, f32[208,128]{1,0:T(8,128)S(1)}, u32[]{:S(2)}, u32[]{:S(2)}) %collective-permute-start.4) | collective-permute-done | bytes 106528 | tf_op jit(solution)/shard_map/ppermute | solution.py:52
  35.9 2.5 %collective-permute-start.8 = (f32[80,128]{1,0:T(8,128)S(1)}, f32[80,128]{1,0:T(8,128)S(1)}, u32[]{:S(2)}, u32[]{:S(2)}) collective-permute-start(f32[80,128]{1,0:T(8,128)S(1)} %get-tuple-element.20), channel_id=1, source_target_pairs={{0,6},{1,7},{2,0},{3,1},{4,2},{5,3},{6,4},{7,5},{8,14},{9,15},{10,... | collective-permute-start | bytes 122888 | tf_op jit(solution)/shard_map/ppermute | solution.py:52
  38.5 1.7 %collective-permute-start.6 = (f32[80,128]{1,0:T(8,128)S(1)}, f32[80,128]{1,0:T(8,128)S(1)}, u32[]{:S(2)}, u32[]{:S(2)}) collective-permute-start(f32[80,128]{1,0:T(8,128)S(1)} %get-tuple-element.20), channel_id=1, source_target_pairs={{0,4},{1,5},{2,6},{3,7},{4,0},{5,1},{6,2},{7,3},{8,12},{9,13},{10,... | collective-permute-start | bytes 122888 | tf_op jit(solution)/shard_map/ppermute | solution.py:52
  40.2 2.8 %collective-permute-done.7 = f32[80,128]{1,0:T(8,128)S(1)} collective-permute-done((f32[80,128]{1,0:T(8,128)S(1)}, f32[80,128]{1,0:T(8,128)S(1)}, u32[]{:S(2)}, u32[]{:S(2)}) %collective-permute-start.7) | collective-permute-done | bytes 40992 | tf_op jit(solution)/shard_map/ppermute | solution.py:52
  43.0 5.0 %collective-permute-start.9 = (f32[80,128]{1,0:T(8,128)S(1)}, f32[80,128]{1,0:T(8,128)S(1)}, u32[]{:S(2)}, u32[]{:S(2)}) collective-permute-start(f32[80,128]{1,0:T(8,128)S(1)} %add_add_fusion), channel_id=1, source_target_pairs={{0,1},{1,0},{2,3},{3,2},{4,5},{5,4},{6,7},{7,6},{8,9},{9,8},{10,11... | collective-permute-start | bytes 122888 | tf_op jit(solution)/shard_map/ppermute | solution.py:52
  48.0 0.9 collective-permute-done.9
  48.9 1.9 %collective-permute-start.12 = (f32[80,128]{1,0:T(8,128)S(1)}, f32[80,128]{1,0:T(8,128)S(1)}, u32[]{:S(2)}, u32[]{:S(2)}) collective-permute-start(f32[80,128]{1,0:T(8,128)S(1)} %add.15), channel_id=1, source_target_pairs={{0,96},{1,25},{2,98},{3,27},{4,100},{5,29},{6,102},{7,31},{8,104},... | collective-permute-start | bytes 122888 | tf_op jit(solution)/shard_map/ppermute | solution.py:52
  50.8 1.1 %collective-permute-start.11 = (f32[80,128]{1,0:T(8,128)S(1)}, f32[80,128]{1,0:T(8,128)S(1)}, u32[]{:S(2)}, u32[]{:S(2)}) collective-permute-start(f32[80,128]{1,0:T(8,128)S(1)} %add.15), channel_id=1, source_target_pairs={{0,64},{1,17},{2,66},{3,19},{4,68},{5,21},{6,70},{7,23},{8,72},{9,... | collective-permute-start | bytes 122888 | tf_op jit(solution)/shard_map/ppermute | solution.py:52
  52.0 3.1 %collective-permute-done.11 = f32[80,128]{1,0:T(8,128)S(1)} collective-permute-done((f32[80,128]{1,0:T(8,128)S(1)}, f32[80,128]{1,0:T(8,128)S(1)}, u32[]{:S(2)}, u32[]{:S(2)}) %collective-permute-start.11) | collective-permute-done | bytes 40992 | tf_op jit(solution)/shard_map/ppermute | solution.py:52
  55.2 0.8 collective-permute-done.10
  56.0 2.3 %collective-permute-start.15 = (f32[320,128]{1,0:T(8,128)S(1)}, f32[320,128]{1,0:T(8,128)S(1)}, u32[]{:S(2)}, u32[]{:S(2)}) collective-permute-start(f32[320,128]{1,0:T(8,128)S(1)} %pad_maximum_fusion.p0), channel_id=1, source_target_pairs={{0,24},{1,97},{2,26},{3,99},{4,28},{5,101},{6,30},{7,103},{8,0},{9... | collective-permute-start | bytes 491528 | tf_op jit(solution)/shard_map/ppermute | solution.py:52
  59.0 3.3 %collective-permute-done.15.p3 = f32[320,128]{1,0:T(8,128)S(1)} collective-permute-done((f32[320,128]{1,0:T(8,128)S(1)}, f32[320,128]{1,0:T(8,128)S(1)}, u32[]{:S(2)}, u32[]{:S(2)}) %collective-permute-start.15) | collective-permute-done | bytes 163872 | tf_op jit(solution)/shard_map/ppermute | solution.py:52
  62.4 1.8 %collective-permute-done.14.p2 = f32[320,128]{1,0:T(8,128)S(1)} collective-permute-done((f32[320,128]{1,0:T(8,128)S(1)}, f32[320,128]{1,0:T(8,128)S(1)}, u32[]{:S(2)}, u32[]{:S(2)}) %collective-permute-start.14) | collective-permute-done | bytes 163872 | tf_op jit(solution)/shard_map/ppermute | solution.py:52
  64.1 1.7 %collective-permute-done.13.p1 = f32[320,128]{1,0:T(8,128)S(1)} collective-permute-done((f32[320,128]{1,0:T(8,128)S(1)}, f32[320,128]{1,0:T(8,128)S(1)}, u32[]{:S(2)}, u32[]{:S(2)}) %collective-permute-start.13) | collective-permute-done | bytes 163872 | tf_op jit(solution)/shard_map/ppermute | solution.py:52
  65.8 32.1 %iterate.1 = (f32[256,32,128]{2,1,0:T(8,128)}, f32[512,128]{1,0:T(8,128)}) custom-call(f32[320,128]{1,0:T(8,128)S(1)} %pad_maximum_fusion.p0, f32[320,128]{1,0:T(8,128)S(1)} %collective-permute-done.13.p1, f32[320,128]{1,0:T(8,128)S(1)} %collective-permute-done.14.p2, f32[320,128]{1,0:T(8,128)S(1)} %collective-permute-done.15.p3, f32[512,128]{1,0:T(8,128)S(1)} %copy-done, ...), custom_call_target="tpu_custom_call" | custom-call | tf_op jit(solution)/shard_map/iterate/pallas_call | solution.py:304
  (17 shorter events, 2.8 us)
Async XLA Ops:
  0.6 65.2 %copy-start = (f32[512,128]{1,0:T(8,128)S(1)}, f32[512,128]{1,0:T(8,128)}, u32[]{:S(2)}) copy-start(f32[512,128]{1,0:T(8,128)} %start_ref.1) | copy-start | bytes 786436
  15.1 7.3 %collective-permute-start = (f32[448,128]{1,0:T(8,128)S(1)}, f32[448,128]{1,0:T(8,128)S(1)}, u32[]{:S(2)}, u32[]{:S(2)}) collective-permute-start(f32[448,128]{1,0:T(8,128)S(1)} %get-tuple-element.13), channel_id=1, source_target_pairs={{0,8},{1,33},{2,10},{3,35},{4,12},{5,37},{6,14},{7,39},{8,16},{9,4... | collective-permute-start | bytes 688136 | tf_op jit(solution)/shard_map/ppermute | solution.py:52
  17.3 8.8 %collective-permute-start.1 = (f32[448,128]{1,0:T(8,128)S(1)}, f32[448,128]{1,0:T(8,128)S(1)}, u32[]{:S(2)}, u32[]{:S(2)}) collective-permute-start(f32[448,128]{1,0:T(8,128)S(1)} %get-tuple-element.14), channel_id=1, source_target_pairs={{0,16},{1,65},{2,18},{3,67},{4,20},{5,69},{6,22},{7,71},{8,24},{9,... | collective-permute-start | bytes 688136 | tf_op jit(solution)/shard_map/ppermute | solution.py:52
  20.0 6.2 %collective-permute-start.2 = (f32[448,128]{1,0:T(8,128)S(1)}, f32[448,128]{1,0:T(8,128)S(1)}, u32[]{:S(2)}, u32[]{:S(2)}) collective-permute-start(f32[448,128]{1,0:T(8,128)S(1)} %get-tuple-element.15), channel_id=1, source_target_pairs={{0,24},{1,97},{2,26},{3,99},{4,28},{5,101},{6,30},{7,103},{8,0},{9... | collective-permute-start | bytes 688136 | tf_op jit(solution)/shard_map/ppermute | solution.py:52
  26.9 5.6 %collective-permute-start.3 = (f32[208,128]{1,0:T(8,128)S(1)}, f32[208,128]{1,0:T(8,128)S(1)}, u32[]{:S(2)}, u32[]{:S(2)}) collective-permute-start(f32[208,128]{1,0:T(8,128)S(1)} %get-tuple-element.17), channel_id=1, source_target_pairs={{0,32},{1,9},{2,34},{3,11},{4,36},{5,13},{6,38},{7,15},{8,40},{9,1... | collective-permute-start | bytes 319496 | tf_op jit(solution)/shard_map/ppermute | solution.py:52
  28.3 6.5 %collective-permute-start.4 = (f32[208,128]{1,0:T(8,128)S(1)}, f32[208,128]{1,0:T(8,128)S(1)}, u32[]{:S(2)}, u32[]{:S(2)}) collective-permute-start(f32[208,128]{1,0:T(8,128)S(1)} %get-tuple-element.18), channel_id=1, source_target_pairs={{0,64},{1,17},{2,66},{3,19},{4,68},{5,21},{6,70},{7,23},{8,72},{9,... | collective-permute-start | bytes 319496 | tf_op jit(solution)/shard_map/ppermute | solution.py:52
  31.6 3.6 %collective-permute-start.5 = (f32[208,128]{1,0:T(8,128)S(1)}, f32[208,128]{1,0:T(8,128)S(1)}, u32[]{:S(2)}, u32[]{:S(2)}) collective-permute-start(f32[208,128]{1,0:T(8,128)S(1)} %get-tuple-element.19), channel_id=1, source_target_pairs={{0,96},{1,25},{2,98},{3,27},{4,100},{5,29},{6,102},{7,31},{8,104},... | collective-permute-start | bytes 319496 | tf_op jit(solution)/shard_map/ppermute | solution.py:52
  35.9 4.3 %collective-permute-start.8 = (f32[80,128]{1,0:T(8,128)S(1)}, f32[80,128]{1,0:T(8,128)S(1)}, u32[]{:S(2)}, u32[]{:S(2)}) collective-permute-start(f32[80,128]{1,0:T(8,128)S(1)} %get-tuple-element.20), channel_id=1, source_target_pairs={{0,6},{1,7},{2,0},{3,1},{4,2},{5,3},{6,4},{7,5},{8,14},{9,15},{10,... | collective-permute-start | bytes 122888 | tf_op jit(solution)/shard_map/ppermute | solution.py:52
  38.5 4.5 %collective-permute-start.7 = (f32[80,128]{1,0:T(8,128)S(1)}, f32[80,128]{1,0:T(8,128)S(1)}, u32[]{:S(2)}, u32[]{:S(2)}) collective-permute-start(f32[80,128]{1,0:T(8,128)S(1)} %get-tuple-element.20), channel_id=1, source_target_pairs={{0,2},{1,3},{2,4},{3,5},{4,6},{5,7},{6,0},{7,1},{8,10},{9,11},{10,... | collective-permute-start | bytes 122888 | tf_op jit(solution)/shard_map/ppermute | solution.py:52
  38.5 4.5 %collective-permute-start.6 = (f32[80,128]{1,0:T(8,128)S(1)}, f32[80,128]{1,0:T(8,128)S(1)}, u32[]{:S(2)}, u32[]{:S(2)}) collective-permute-start(f32[80,128]{1,0:T(8,128)S(1)} %get-tuple-element.20), channel_id=1, source_target_pairs={{0,4},{1,5},{2,6},{3,7},{4,0},{5,1},{6,2},{7,3},{8,12},{9,13},{10,... | collective-permute-start | bytes 122888 | tf_op jit(solution)/shard_map/ppermute | solution.py:52
  43.0 5.9 %collective-permute-start.9 = (f32[80,128]{1,0:T(8,128)S(1)}, f32[80,128]{1,0:T(8,128)S(1)}, u32[]{:S(2)}, u32[]{:S(2)}) collective-permute-start(f32[80,128]{1,0:T(8,128)S(1)} %add_add_fusion), channel_id=1, source_target_pairs={{0,1},{1,0},{2,3},{3,2},{4,5},{5,4},{6,7},{7,6},{8,9},{9,8},{10,11... | collective-permute-start | bytes 122888 | tf_op jit(solution)/shard_map/ppermute | solution.py:52
  48.9 3.1 %collective-permute-start.12 = (f32[80,128]{1,0:T(8,128)S(1)}, f32[80,128]{1,0:T(8,128)S(1)}, u32[]{:S(2)}, u32[]{:S(2)}) collective-permute-start(f32[80,128]{1,0:T(8,128)S(1)} %add.15), channel_id=1, source_target_pairs={{0,96},{1,25},{2,98},{3,27},{4,100},{5,29},{6,102},{7,31},{8,104},... | collective-permute-start | bytes 122888 | tf_op jit(solution)/shard_map/ppermute | solution.py:52
  50.8 4.4 %collective-permute-start.11 = (f32[80,128]{1,0:T(8,128)S(1)}, f32[80,128]{1,0:T(8,128)S(1)}, u32[]{:S(2)}, u32[]{:S(2)}) collective-permute-start(f32[80,128]{1,0:T(8,128)S(1)} %add.15), channel_id=1, source_target_pairs={{0,64},{1,17},{2,66},{3,19},{4,68},{5,21},{6,70},{7,23},{8,72},{9,... | collective-permute-start | bytes 122888 | tf_op jit(solution)/shard_map/ppermute | solution.py:52
  51.9 4.1 %collective-permute-start.10 = (f32[80,128]{1,0:T(8,128)S(1)}, f32[80,128]{1,0:T(8,128)S(1)}, u32[]{:S(2)}, u32[]{:S(2)}) collective-permute-start(f32[80,128]{1,0:T(8,128)S(1)} %add.15), channel_id=1, source_target_pairs={{0,32},{1,9},{2,34},{3,11},{4,36},{5,13},{6,38},{7,15},{8,40},{9,1... | collective-permute-start | bytes 122888 | tf_op jit(solution)/shard_map/ppermute | solution.py:52
  56.0 6.4 %collective-permute-start.15 = (f32[320,128]{1,0:T(8,128)S(1)}, f32[320,128]{1,0:T(8,128)S(1)}, u32[]{:S(2)}, u32[]{:S(2)}) collective-permute-start(f32[320,128]{1,0:T(8,128)S(1)} %pad_maximum_fusion.p0), channel_id=1, source_target_pairs={{0,24},{1,97},{2,26},{3,99},{4,28},{5,101},{6,30},{7,103},{8,0},{9... | collective-permute-start | bytes 491528 | tf_op jit(solution)/shard_map/ppermute | solution.py:52
  58.4 5.8 %collective-permute-start.14 = (f32[320,128]{1,0:T(8,128)S(1)}, f32[320,128]{1,0:T(8,128)S(1)}, u32[]{:S(2)}, u32[]{:S(2)}) collective-permute-start(f32[320,128]{1,0:T(8,128)S(1)} %pad_maximum_fusion.p0), channel_id=1, source_target_pairs={{0,16},{1,65},{2,18},{3,67},{4,20},{5,69},{6,22},{7,71},{8,24},{9,... | collective-permute-start | bytes 491528 | tf_op jit(solution)/shard_map/ppermute | solution.py:52
  58.4 7.4 %collective-permute-start.13 = (f32[320,128]{1,0:T(8,128)S(1)}, f32[320,128]{1,0:T(8,128)S(1)}, u32[]{:S(2)}, u32[]{:S(2)}) collective-permute-start(f32[320,128]{1,0:T(8,128)S(1)} %pad_maximum_fusion.p0), channel_id=1, source_target_pairs={{0,8},{1,33},{2,10},{3,35},{4,12},{5,37},{6,14},{7,39},{8,16},{9,4... | collective-permute-start | bytes 491528 | tf_op jit(solution)/shard_map/ppermute | solution.py:52

commit v2 on v1

--- a/solution.py
+++ b/solution.py
@@ -58,74 +58,97 @@
     )
 
 
-def gram_kernel(x_ref, *refs):
-    outs, (split, top, low, shift, total, packed) = refs[:4], refs[4:]
-    step = pl.program_id(0)
-
-    @pl.when(step == 0)
-    def _():
-        shift[...] = jnp.sum(x_ref[...], axis=0) * (1.0 / CHUNK)
-        total[...] = jnp.zeros_like(total)
-        top[...] = jnp.zeros_like(top)
-        low[...] = jnp.zeros_like(low)
-
-    d = x_ref[...] - shift[...][None]
-    total[...] += jnp.sum(d, axis=0)
-    d = d.reshape(CHUNK * GENS, LOCI)
-    hi = d.astype(jnp.bfloat16)
-    split[:, :LOCI] = hi
-    split[:, LOCI:] = (d - hi.astype(jnp.float32)).astype(jnp.bfloat16)
-    top[...] += cross(split[:, :256], split[...])
-    low[...] += cross(split[:, 256:512], split[:, 256:])
-
-    @pl.when(step == pl.num_programs(0) - 1)
-    def _():
-        sums = total[...]
-        offset = cross(sums, sums, lax.Precision.HIGHEST) * (1.0 / DEMES)
-
-        def high(i, j):
-            if i < 2:
-                return top[BLOCK * i : BLOCK * (i + 1), BLOCK * j : BLOCK * (j + 1)]
-            return low[BLOCK * (i - 2) : BLOCK * (i - 1), BLOCK * (j - 2) : BLOCK * (j - 1)]
-
-        def mixed(i, j):
-            if i < 2:
-                return top[BLOCK * i : BLOCK * (i + 1), LOCI + BLOCK * j : LOCI + BLOCK * (j + 1)]
-            return low[BLOCK * (i - 2) : BLOCK * (i - 1), 256 + BLOCK * j : 256 + BLOCK * (j + 1)]
-
-        for n, (i, j) in enumerate(PAIRS):
-            block = high(i, j) + (mixed(i, j) + mixed(j, i).T)
-            packed[BLOCK * n : BLOCK * (n + 1), :] = (
-                block - offset[BLOCK * i : BLOCK * (i + 1), BLOCK * j : BLOCK * (j + 1)]
-            )
-        mean = shift[...] + sums * (1.0 / DEMES)
-        first, second, core = place()
-        for k, out in enumerate(outs):
-            to = (first + k) % 4
-            for j in range(4):
-                row = pl.multiple_of(piece_row(core, to, j), 8)
-                out[PIECE * j : PIECE * (j + 1), :] = packed[pl.ds(row, PIECE), :]
-                out[4 * PIECE + 32 * j : 4 * PIECE + 32 * (j + 1), :] = mean[:, BLOCK * j : BLOCK * (j + 1)]
+def halves(value):
+    hi = value.astype(jnp.bfloat16)
+    return hi, (value - hi.astype(jnp.float32)).astype(jnp.bfloat16)
+
+
+def gram_of_few(value, columns):
+    hi, lo = halves(value)
+    left = jnp.concatenate([hi, hi, lo], axis=0)
+    right = jnp.concatenate([hi, lo, hi], axis=0)
+    return cross(left[:, columns], right[:, columns.start :])
+
+
+def gram_kernel(x_hbm, *refs):
+    outs, (x, halved, top, low, shift, total, packed, loads) = refs[:4], refs[4:]
+    chunks = DEMES // CHUNK
+
+    def load(n):
+        part = pl.ds(n * CHUNK, CHUNK)
+        return pltpu.make_async_copy(x_hbm.at[part], x.at[part], loads.at[n])
+
+    def split(n, to):
+        d = x[pl.ds(n * CHUNK, CHUNK)] - shift[...][None]
+        total[...] += jnp.sum(d, axis=0)
+        to[:, LOCI:], to[:, :LOCI] = halves(d.reshape(CHUNK * GENS, LOCI))
+
+    def multiply(part):
+        top_part = cross(part[:, :768], part[:, 512:768])
+        low_part = cross(part[...], part[:, 768:])
+        top[...] += top_part
+        low[...] += low_part
+
+    for n in range(chunks):
+        load(n).start()
+    total[...] = jnp.zeros_like(total)
+    top[...] = jnp.zeros_like(top)
+    low[...] = jnp.zeros_like(low)
+    load(0).wait()
+    shift[...] = jnp.sum(x[:CHUNK], axis=0) * (1.0 / CHUNK)
+    split(0, halved)
+    multiply(halved)
+
+    def body(n, carry):
+        load(n).wait()
+        split(n, halved)
+        multiply(halved)
+        return carry
+
+    lax.fori_loop(1, chunks, body, 0)
+
+    sums = total[...]
+
+    def part(first_row, i, j):
+        rows = slice(first_row + BLOCK * i, first_row + BLOCK * (i + 1))
+        if j < 2:
+            return top[rows, BLOCK * j : BLOCK * (j + 1)]
+        return low[rows, BLOCK * (j - 2) : BLOCK * (j - 1)]
+
+    for i in range(4):
+        offset = gram_of_few(sums, slice(BLOCK * i, BLOCK * (i + 1))) * (1.0 / DEMES)
+        for j in range(i, 4):
+            n = PAIRS.index((i, j))
+            block = part(LOCI, i, j) + (part(0, i, j) + part(0, j, i).T)
+            packed[BLOCK * n : BLOCK * (n + 1), :] = block - offset[:, BLOCK * (j - i) : BLOCK * (j - i + 1)]
+    mean = shift[...] + sums * (1.0 / DEMES)
+    first, second, core = place()
+    for k, out in enumerate(outs):
+        to = (first + k) % 4
+        for j in range(4):
+            row = pl.multiple_of(piece_row(core, to, j), 8)
+            out[PIECE * j : PIECE * (j + 1), :] = packed[pl.ds(row, PIECE), :]
+            out[4 * PIECE + 32 * j : 4 * PIECE + 32 * (j + 1), :] = mean[:, BLOCK * j : BLOCK * (j + 1)]
 
 
 def local_gram(freqs):
     rows = 4 * PIECE + MEAN_ROWS
     return pl.pallas_call(
         gram_kernel,
-        grid=(DEMES // CHUNK,),
-        in_specs=[pl.BlockSpec((CHUNK, GENS, LOCI), lambda t: (t, 0, 0))],
-        out_specs=[pl.BlockSpec((rows, BLOCK), lambda t: (0, 0))] * 4,
+        in_specs=[pl.BlockSpec(memory_space=pltpu.HBM)],
+        out_specs=[pl.BlockSpec(memory_space=pltpu.VMEM)] * 4,
         out_shape=[jax.ShapeDtypeStruct((rows, BLOCK), jnp.float32)] * 4,
         scratch_shapes=[
+            pltpu.VMEM((DEMES, GENS, LOCI), jnp.float32),
             pltpu.VMEM((CHUNK * GENS, 2 * LOCI), jnp.bfloat16),
-            pltpu.VMEM((256, 1024), jnp.float32),
-            pltpu.VMEM((256, 768), jnp.float32),
+            pltpu.VMEM((768, 256), jnp.float32),
+            pltpu.VMEM((1024, 256), jnp.float32),
             pltpu.VMEM((GENS, LOCI), jnp.float32),
             pltpu.VMEM((GENS, LOCI), jnp.float32),
             pltpu.VMEM((PACKED, BLOCK), jnp.float32),
+            pltpu.SemaphoreType.DMA((DEMES // CHUNK,)),
         ],
-        compiler_params=pltpu.CompilerParams(vmem_limit_bytes=40 * MIB),
-        cost_estimate=pl.CostEstimate(flops=2 * 8192 * 512 * 900, bytes_accessed=20 * MIB, transcendentals=0),
+        compiler_params=pltpu.CompilerParams(vmem_limit_bytes=48 * MIB),
         name="local_gram",
     )(freqs)
 
@@ -137,7 +160,7 @@
     mean = ((wide[0] + wide[2]) + (wide[1] + wide[3])) * 0.25
     delta = jnp.concatenate([part - mean for part in wide], axis=0)
     for i in range(4):
-        product = cross(delta[:, BLOCK * i : BLOCK * (i + 1)], delta[:, BLOCK * i :], lax.Precision.HIGHEST)
+        product = gram_of_few(delta, slice(BLOCK * i, BLOCK * (i + 1)))
         for j in range(i, 4):
             n = PAIRS.index((i, j))
             packed[BLOCK * n : BLOCK * (n + 1), :] = product[:, BLOCK * (j - i) : BLOCK * (j - i + 1)] * weight
@@ -202,36 +225,51 @@
     sub = lax.broadcasted_iota(jnp.int32, full, 0)
     count = RANK // 8
     rows = [s[8 * i : 8 * i + 8, :] for i in range(count)]
+
+    def spread_row(value, j):
+        return jnp.broadcast_to(value[j : j + 1, :], full)
+
+    def spread_columns(i, k):
+        return [jnp.broadcast_to(rows[i][:, 8 * k + j : 8 * k + j + 1], full) for j in range(8)]
+
+    own_columns = spread_columns(0, 0)
     for k in range(count):
-        cols = {
-            i: [jnp.broadcast_to(rows[i][:, 8 * k + j : 8 * k + j + 1], full) for j in range(8)]
-            for i in range(k, count)
-        }
-        inverses = []
-        for j in range(8):
-            pivot = cols[k][j]
-            inverse = 1.0 / jnp.broadcast_to(pivot[j : j + 1, :], full)
-            inverses.append(inverse)
-            for l in range(j + 1, 8):
-                ratio = jnp.broadcast_to(pivot[l : l + 1, :], full) * inverse
-                for i in range(k, count):
-                    cols[i][l] = cols[i][l] - cols[i][j] * ratio
         here = (lane >= 8 * k) & (lane < 8 * k + 8)
         own = jnp.where(here, jnp.where(lane - 8 * k == sub, 1.0, 0.0), rows[k])
-        scaled = []
-        scale = inverses[0]
+        last = k == count - 1
+        if not last:
+            near = spread_columns(k + 1, k)
+            after = spread_columns(k + 1, k + 1)
+            near_rows = jnp.where(here, 0.0, rows[k + 1])
+        ratio, scaled, scale = {}, [], None
         for j in range(8):
-            scaled.append(jnp.broadcast_to(own[j : j + 1, :], full) * inverses[j])
+            inverse = 1.0 / spread_row(own_columns[j], j)
+            for l in range(j + 1, 8):
+                ratio[l, j] = spread_row(own_columns[j], l) * inverse
+                own_columns[l] = own_columns[l] - own_columns[j] * ratio[l, j]
+            scaled.append(spread_row(own, j) * inverse)
             if j < 7:
-                own = own - jnp.where(sub > j, cols[k][j], 0.0) * scaled[j]
-            if j:
-                scale = jnp.where(sub == j, inverses[j], scale)
-        for i in range(k + 1, count):
-            rest = jnp.where(here, 0.0, rows[i])
-            for j in range(8):
-                rest = rest - cols[i][j] * scaled[j]
-            rows[i] = rest
+                own = own - jnp.where(sub > j, own_columns[j], 0.0) * scaled[j]
+            scale = jnp.where(sub == j, inverse, scale) if j else inverse
+            if not last:
+                near_rows = near_rows - near[j] * scaled[j]
+                for l in range(8):
+                    after[l] = after[l] - near[j] * (spread_row(near[j], l) * inverse)
+                for l in range(j + 1, 8):
+                    near[l] = near[l] - near[j] * ratio[l, j]
+        solved = list(scaled)
+        for j in range(7, 0, -1):
+            for m in range(j):
+                solved[m] = solved[m] - ratio[j, m] * solved[j]
+        for i in range(k + 2, count):
+            t = [column * part for column, part in zip(spread_columns(i, k), solved)]
+            rows[i] = jnp.where(here, 0.0, rows[i]) - (
+                ((t[0] + t[1]) + (t[2] + t[3])) + ((t[4] + t[5]) + (t[6] + t[7]))
+            )
         rows[k] = jnp.where(lane <= 8 * k + sub, own * jnp.sqrt(scale), 0.0)
+        if not last:
+            rows[k + 1] = near_rows
+            own_columns = after
     return jnp.concatenate(rows, axis=0)
 
 
@@ -240,7 +278,10 @@
 LOADS = 4
 
 
-def core_kernel(p0, p1, p2, p3, start_ref, mean_ref, x_hbm, core_hbm, factor_ref, x, core, packed, gram, loads, stores):
+def core_kernel(
+    p0, p1, p2, p3, start_ref, mean_ref, x_hbm, core_hbm, factor_ref,
+    x, core, packed, gram, both, hi_a, lo_a, hi_b, lo_b, loads, stores,
+):
     def load(n):
         part = pl.ds(n * (DEMES // LOADS), DEMES // LOADS)
         return pltpu.make_async_copy(x_hbm.at[part], x.at[part], loads.at[n])
@@ -276,24 +317,32 @@
     factor = basis.T
     factor_ref[...] = factor
     hi = factor.astype(jnp.bfloat16)
-    lo = (factor - hi.astype(jnp.float32)).astype(jnp.bfloat16)
-    both = jnp.concatenate([hi, lo], axis=1)
-    mean = mean_ref[...]
+    both[:, :RANK] = hi
+    both[:, RANK:] = (factor - hi.astype(jnp.float32)).astype(jnp.bfloat16)
     for n in range(LOADS):
         load(n).wait()
 
-    def step(n, carry):
-        part = pl.ds(n * STEP, STEP)
-        d = (x[part] - mean[None]).reshape(STEP * GENS, LOCI)
-        d_hi = d.astype(jnp.bfloat16)
-        d_lo = (d - d_hi.astype(jnp.float32)).astype(jnp.bfloat16)
-        wide = jnp.dot(d_hi, both, preferred_element_type=jnp.float32)
-        rest = jnp.dot(d_lo, hi, preferred_element_type=jnp.float32)
-        core[part] = (wide[:, :RANK] + (wide[:, RANK:] + rest)).reshape(STEP, GENS, RANK)
-        store(n).start()
+    def split(n, d_hi, d_lo):
+        d = (x[pl.ds(n * STEP, STEP)] - mean_ref[...][None]).reshape(STEP * GENS, LOCI)
+        d_hi[...] = d.astype(jnp.bfloat16)
+        d_lo[...] = (d - d.astype(jnp.bfloat16).astype(jnp.float32)).astype(jnp.bfloat16)
+
+    def multiply(n, d_hi, d_lo):
+        wide = jnp.dot(d_hi[...], both[...], preferred_element_type=jnp.float32)
+        rest = jnp.dot(d_lo[...], both[:, :RANK], preferred_element_type=jnp.float32)
+        core[pl.ds(n * STEP, STEP)] = (wide[:, :RANK] + (wide[:, RANK:] + rest)).reshape(STEP, GENS, RANK)
+
+    def pair(p, carry):
+        split(2 * p + 1, hi_b, lo_b)
+        multiply(2 * p, hi_a, lo_a)
+        split(jnp.minimum(2 * p + 2, STEPS - 1), hi_a, lo_a)
+        multiply(2 * p + 1, hi_b, lo_b)
+        store(2 * p).start()
+        store(2 * p + 1).start()
         return carry
 
-    lax.fori_loop(0, STEPS, step, 0)
+    split(0, hi_a, lo_a)
+    lax.fori_loop(0, STEPS // 2, pair, 0)
     for n in range(STEPS):
         store(n).wait()
 
@@ -314,6 +363,10 @@
             pltpu.VMEM((DEMES, GENS, RANK), jnp.float32),
             pltpu.VMEM((PACKED, BLOCK), jnp.float32),
             pltpu.VMEM((LOCI, LOCI), jnp.float32),
+            pltpu.VMEM((LOCI, 2 * RANK), jnp.bfloat16),
+        ]
+        + [pltpu.VMEM((STEP * GENS, LOCI), jnp.bfloat16)] * 4
+        + [
             pltpu.SemaphoreType.DMA((LOADS,)),
             pltpu.SemaphoreType.DMA((STEPS,)),
         ],

time: 99.9 us -> 91.2 us (0.913)
  Pallas kernels: 48.1 us -> 39.6 us
    pallas_call x1, Pallas kernels: 32.1 us -> 26.6 us  [iterate(): pl.pallas_call(core_kernel, in_specs=[vmem] * 6 + [hbm], out_specs=[hbm,...]
    pallas_call x1, Pallas kernels: 14.5 us -> 12.2 us  [local_gram(): pl.pallas_call(gram_kernel, in_specs=[pl.BlockSpec(memory_space=pltpu.HBM...]
where the time goes in v2:
time: 91.2 us; the launch traced here: 89.5 us
  Pallas kernels  39.6 us (43%)
  starting transfers between devices  26.7 us (29%)
  waiting for transfers between devices  22.3 us (24%)
    ppermute x16, starting transfers between devices, send(): return lax.ppermute(value, AXES, shifted(kind, k))  26.7 us
    pallas_call x1, Pallas kernels, iterate(): pl.pallas_call(core_kernel, in_specs=[vmem] * 6 + [hbm], out_specs=[hbm,...  26.6 us
    ppermute x16, waiting for transfers between devices, send(): return lax.ppermute(value, AXES, shifted(kind, k))  22.3 us
    pallas_call x1, Pallas kernels, local_gram(): pl.pallas_call(gram_kernel, in_specs=[pl.BlockSpec(memory_space=pltpu.HBM...  12.2 us
  transfers between devices with their start and end apart: 16, of which 12 were waited for; matrix products, arithmetic and copies ran while one was open for 0% of the time, Pallas kernels for 0%

profile of v2, /device:TPU:1, one launch (start us, length us, event | category | flops | bytes accessed | tf_op | source)
XLA Modules:
  0.0 89.5 jit_solution(3260433294950797458)
XLA Ops:
  0.6 12.2 %local_gram.1 = (f32[448,128]{1,0:T(8,128)S(1)}, f32[448,128]{1,0:T(8,128)S(1)}, f32[448,128]{1,0:T(8,128)S(1)}, f32[448,128]{1,0:T(8,128)S(1)}) custom-call(f32[256,32,512]{2,1,0:T(8,128)} %x_hbm.3), custom_call_target="tpu_custom_call" | custom-call | tf_op jit(solution)/shard_map/local_gram/pallas_call | solution.py:136
  12.8 2.2 %collective-permute-start = (f32[448,128]{1,0:T(8,128)S(1)}, f32[448,128]{1,0:T(8,128)S(1)}, u32[]{:S(2)}, u32[]{:S(2)}) collective-permute-start(f32[448,128]{1,0:T(8,128)S(1)} %get-tuple-element.13), channel_id=1, source_target_pairs={{0,8},{1,33},{2,10},{3,35},{4,12},{5,37},{6,14},{7,39},{8,16},{9,4... | collective-permute-start | bytes 688136 | tf_op jit(solution)/shard_map/ppermute | solution.py:52
  15.0 2.6 %collective-permute-start.1 = (f32[448,128]{1,0:T(8,128)S(1)}, f32[448,128]{1,0:T(8,128)S(1)}, u32[]{:S(2)}, u32[]{:S(2)}) collective-permute-start(f32[448,128]{1,0:T(8,128)S(1)} %get-tuple-element.14), channel_id=1, source_target_pairs={{0,16},{1,65},{2,18},{3,67},{4,20},{5,69},{6,22},{7,71},{8,24},{9,... | collective-permute-start | bytes 688136 | tf_op jit(solution)/shard_map/ppermute | solution.py:52
  17.6 1.1 %collective-permute-start.2 = (f32[448,128]{1,0:T(8,128)S(1)}, f32[448,128]{1,0:T(8,128)S(1)}, u32[]{:S(2)}, u32[]{:S(2)}) collective-permute-start(f32[448,128]{1,0:T(8,128)S(1)} %get-tuple-element.15), channel_id=1, source_target_pairs={{0,24},{1,97},{2,26},{3,99},{4,28},{5,101},{6,30},{7,103},{8,0},{9... | collective-permute-start | bytes 688136 | tf_op jit(solution)/shard_map/ppermute | solution.py:52
  18.7 1.5 %collective-permute-done.refs_1_ = f32[448,128]{1,0:T(8,128)S(1)} collective-permute-done((f32[448,128]{1,0:T(8,128)S(1)}, f32[448,128]{1,0:T(8,128)S(1)}, u32[]{:S(2)}, u32[]{:S(2)}) %collective-permute-start) | collective-permute-done | bytes 229408 | tf_op jit(solution)/shard_map/ppermute | solution.py:52
  20.2 3.6 %collective-permute-done.1.refs_2_ = f32[448,128]{1,0:T(8,128)S(1)} collective-permute-done((f32[448,128]{1,0:T(8,128)S(1)}, f32[448,128]{1,0:T(8,128)S(1)}, u32[]{:S(2)}, u32[]{:S(2)}) %collective-permute-start.1) | collective-permute-done | bytes 229408 | tf_op jit(solution)/shard_map/ppermute | solution.py:52
  24.2 1.4 %collective-permute-start.3 = (f32[208,128]{1,0:T(8,128)S(1)}, f32[208,128]{1,0:T(8,128)S(1)}, u32[]{:S(2)}, u32[]{:S(2)}) collective-permute-start(f32[208,128]{1,0:T(8,128)S(1)} %get-tuple-element.17), channel_id=1, source_target_pairs={{0,32},{1,9},{2,34},{3,11},{4,36},{5,13},{6,38},{7,15},{8,40},{9,1... | collective-permute-start | bytes 319496 | tf_op jit(solution)/shard_map/ppermute | solution.py:52
  25.6 3.3 %collective-permute-start.4 = (f32[208,128]{1,0:T(8,128)S(1)}, f32[208,128]{1,0:T(8,128)S(1)}, u32[]{:S(2)}, u32[]{:S(2)}) collective-permute-start(f32[208,128]{1,0:T(8,128)S(1)} %get-tuple-element.18), channel_id=1, source_target_pairs={{0,64},{1,17},{2,66},{3,19},{4,68},{5,21},{6,70},{7,23},{8,72},{9,... | collective-permute-start | bytes 319496 | tf_op jit(solution)/shard_map/ppermute | solution.py:52
  29.0 0.7 collective-permute-start.5
  29.9 2.3 %collective-permute-done.4.refs_2_ = f32[208,128]{1,0:T(8,128)S(1)} collective-permute-done((f32[208,128]{1,0:T(8,128)S(1)}, f32[208,128]{1,0:T(8,128)S(1)}, u32[]{:S(2)}, u32[]{:S(2)}) %collective-permute-start.4) | collective-permute-done | bytes 106528 | tf_op jit(solution)/shard_map/ppermute | solution.py:52
  32.9 2.5 %collective-permute-start.8 = (f32[80,128]{1,0:T(8,128)S(1)}, f32[80,128]{1,0:T(8,128)S(1)}, u32[]{:S(2)}, u32[]{:S(2)}) collective-permute-start(f32[80,128]{1,0:T(8,128)S(1)} %get-tuple-element.20), channel_id=1, source_target_pairs={{0,6},{1,7},{2,0},{3,1},{4,2},{5,3},{6,4},{7,5},{8,14},{9,15},{10,... | collective-permute-start | bytes 122888 | tf_op jit(solution)/shard_map/ppermute | solution.py:52
  35.5 1.7 %collective-permute-start.6 = (f32[80,128]{1,0:T(8,128)S(1)}, f32[80,128]{1,0:T(8,128)S(1)}, u32[]{:S(2)}, u32[]{:S(2)}) collective-permute-start(f32[80,128]{1,0:T(8,128)S(1)} %get-tuple-element.20), channel_id=1, source_target_pairs={{0,4},{1,5},{2,6},{3,7},{4,0},{5,1},{6,2},{7,3},{8,12},{9,13},{10,... | collective-permute-start | bytes 122888 | tf_op jit(solution)/shard_map/ppermute | solution.py:52
  37.2 2.8 %collective-permute-done.7 = f32[80,128]{1,0:T(8,128)S(1)} collective-permute-done((f32[80,128]{1,0:T(8,128)S(1)}, f32[80,128]{1,0:T(8,128)S(1)}, u32[]{:S(2)}, u32[]{:S(2)}) %collective-permute-start.7) | collective-permute-done | bytes 40992 | tf_op jit(solution)/shard_map/ppermute | solution.py:52
  40.0 5.0 %collective-permute-start.9 = (f32[80,128]{1,0:T(8,128)S(1)}, f32[80,128]{1,0:T(8,128)S(1)}, u32[]{:S(2)}, u32[]{:S(2)}) collective-permute-start(f32[80,128]{1,0:T(8,128)S(1)} %add_add_fusion), channel_id=1, source_target_pairs={{0,1},{1,0},{2,3},{3,2},{4,5},{5,4},{6,7},{7,6},{8,9},{9,8},{10,11... | collective-permute-start | bytes 122888 | tf_op jit(solution)/shard_map/ppermute | solution.py:52
  45.0 0.9 collective-permute-done.9
  45.9 1.9 %collective-permute-start.12 = (f32[80,128]{1,0:T(8,128)S(1)}, f32[80,128]{1,0:T(8,128)S(1)}, u32[]{:S(2)}, u32[]{:S(2)}) collective-permute-start(f32[80,128]{1,0:T(8,128)S(1)} %add.15), channel_id=1, source_target_pairs={{0,96},{1,25},{2,98},{3,27},{4,100},{5,29},{6,102},{7,31},{8,104},... | collective-permute-start | bytes 122888 | tf_op jit(solution)/shard_map/ppermute | solution.py:52
  47.8 1.1 %collective-permute-start.11 = (f32[80,128]{1,0:T(8,128)S(1)}, f32[80,128]{1,0:T(8,128)S(1)}, u32[]{:S(2)}, u32[]{:S(2)}) collective-permute-start(f32[80,128]{1,0:T(8,128)S(1)} %add.15), channel_id=1, source_target_pairs={{0,64},{1,17},{2,66},{3,19},{4,68},{5,21},{6,70},{7,23},{8,72},{9,... | collective-permute-start | bytes 122888 | tf_op jit(solution)/shard_map/ppermute | solution.py:52
  49.0 3.1 %collective-permute-done.11 = f32[80,128]{1,0:T(8,128)S(1)} collective-permute-done((f32[80,128]{1,0:T(8,128)S(1)}, f32[80,128]{1,0:T(8,128)S(1)}, u32[]{:S(2)}, u32[]{:S(2)}) %collective-permute-start.11) | collective-permute-done | bytes 40992 | tf_op jit(solution)/shard_map/ppermute | solution.py:52
  52.1 0.8 collective-permute-done.10
  53.0 2.3 %collective-permute-start.15 = (f32[320,128]{1,0:T(8,128)S(1)}, f32[320,128]{1,0:T(8,128)S(1)}, u32[]{:S(2)}, u32[]{:S(2)}) collective-permute-start(f32[320,128]{1,0:T(8,128)S(1)} %pad_maximum_fusion.p0), channel_id=1, source_target_pairs={{0,24},{1,97},{2,26},{3,99},{4,28},{5,101},{6,30},{7,103},{8,0},{9... | collective-permute-start | bytes 491528 | tf_op jit(solution)/shard_map/ppermute | solution.py:52
  56.0 3.3 %collective-permute-done.15.p3 = f32[320,128]{1,0:T(8,128)S(1)} collective-permute-done((f32[320,128]{1,0:T(8,128)S(1)}, f32[320,128]{1,0:T(8,128)S(1)}, u32[]{:S(2)}, u32[]{:S(2)}) %collective-permute-start.15) | collective-permute-done | bytes 163872 | tf_op jit(solution)/shard_map/ppermute | solution.py:52
  59.4 1.8 %collective-permute-done.14.p2 = f32[320,128]{1,0:T(8,128)S(1)} collective-permute-done((f32[320,128]{1,0:T(8,128)S(1)}, f32[320,128]{1,0:T(8,128)S(1)}, u32[]{:S(2)}, u32[]{:S(2)}) %collective-permute-start.14) | collective-permute-done | bytes 163872 | tf_op jit(solution)/shard_map/ppermute | solution.py:52
  61.1 1.7 %collective-permute-done.13.p1 = f32[320,128]{1,0:T(8,128)S(1)} collective-permute-done((f32[320,128]{1,0:T(8,128)S(1)}, f32[320,128]{1,0:T(8,128)S(1)}, u32[]{:S(2)}, u32[]{:S(2)}) %collective-permute-start.13) | collective-permute-done | bytes 163872 | tf_op jit(solution)/shard_map/ppermute | solution.py:52
  62.8 26.6 %iterate.1 = (f32[256,32,128]{2,1,0:T(8,128)}, f32[512,128]{1,0:T(8,128)}) custom-call(f32[320,128]{1,0:T(8,128)S(1)} %pad_maximum_fusion.p0, f32[320,128]{1,0:T(8,128)S(1)} %collective-permute-done.13.p1, f32[320,128]{1,0:T(8,128)S(1)} %collective-permute-done.14.p2, f32[320,128]{1,0:T(8,128)S(1)} %collective-permute-done.15.p3, f32[512,128]{1,0:T(8,128)S(1)} %copy-done, ...), custom_call_target="tpu_custom_call" | custom-call | tf_op jit(solution)/shard_map/iterate/pallas_call | solution.py:353
  (17 shorter events, 2.1 us)
Async XLA Ops:
  0.6 62.2 %copy-start = (f32[512,128]{1,0:T(8,128)S(1)}, f32[512,128]{1,0:T(8,128)}, u32[]{:S(2)}) copy-start(f32[512,128]{1,0:T(8,128)} %start_ref.1) | copy-start | bytes 786436
  12.8 7.3 %collective-permute-start = (f32[448,128]{1,0:T(8,128)S(1)}, f32[448,128]{1,0:T(8,128)S(1)}, u32[]{:S(2)}, u32[]{:S(2)}) collective-permute-start(f32[448,128]{1,0:T(8,128)S(1)} %get-tuple-element.13), channel_id=1, source_target_pairs={{0,8},{1,33},{2,10},{3,35},{4,12},{5,37},{6,14},{7,39},{8,16},{9,4... | collective-permute-start | bytes 688136 | tf_op jit(solution)/shard_map/ppermute | solution.py:52
  15.0 8.8 %collective-permute-start.1 = (f32[448,128]{1,0:T(8,128)S(1)}, f32[448,128]{1,0:T(8,128)S(1)}, u32[]{:S(2)}, u32[]{:S(2)}) collective-permute-start(f32[448,128]{1,0:T(8,128)S(1)} %get-tuple-element.14), channel_id=1, source_target_pairs={{0,16},{1,65},{2,18},{3,67},{4,20},{5,69},{6,22},{7,71},{8,24},{9,... | collective-permute-start | bytes 688136 | tf_op jit(solution)/shard_map/ppermute | solution.py:52
  17.6 6.2 %collective-permute-start.2 = (f32[448,128]{1,0:T(8,128)S(1)}, f32[448,128]{1,0:T(8,128)S(1)}, u32[]{:S(2)}, u32[]{:S(2)}) collective-permute-start(f32[448,128]{1,0:T(8,128)S(1)} %get-tuple-element.15), channel_id=1, source_target_pairs={{0,24},{1,97},{2,26},{3,99},{4,28},{5,101},{6,30},{7,103},{8,0},{9... | collective-permute-start | bytes 688136 | tf_op jit(solution)/shard_map/ppermute | solution.py:52
  24.2 5.6 %collective-permute-start.3 = (f32[208,128]{1,0:T(8,128)S(1)}, f32[208,128]{1,0:T(8,128)S(1)}, u32[]{:S(2)}, u32[]{:S(2)}) collective-permute-start(f32[208,128]{1,0:T(8,128)S(1)} %get-tuple-element.17), channel_id=1, source_target_pairs={{0,32},{1,9},{2,34},{3,11},{4,36},{5,13},{6,38},{7,15},{8,40},{9,1... | collective-permute-start | bytes 319496 | tf_op jit(solution)/shard_map/ppermute | solution.py:52
  25.6 6.5 %collective-permute-start.4 = (f32[208,128]{1,0:T(8,128)S(1)}, f32[208,128]{1,0:T(8,128)S(1)}, u32[]{:S(2)}, u32[]{:S(2)}) collective-permute-start(f32[208,128]{1,0:T(8,128)S(1)} %get-tuple-element.18), channel_id=1, source_target_pairs={{0,64},{1,17},{2,66},{3,19},{4,68},{5,21},{6,70},{7,23},{8,72},{9,... | collective-permute-start | bytes 319496 | tf_op jit(solution)/shard_map/ppermute | solution.py:52
  29.0 3.6 %collective-permute-start.5 = (f32[208,128]{1,0:T(8,128)S(1)}, f32[208,128]{1,0:T(8,128)S(1)}, u32[]{:S(2)}, u32[]{:S(2)}) collective-permute-start(f32[208,128]{1,0:T(8,128)S(1)} %get-tuple-element.19), channel_id=1, source_target_pairs={{0,96},{1,25},{2,98},{3,27},{4,100},{5,29},{6,102},{7,31},{8,104},... | collective-permute-start | bytes 319496 | tf_op jit(solution)/shard_map/ppermute | solution.py:52
  32.9 4.3 %collective-permute-start.8 = (f32[80,128]{1,0:T(8,128)S(1)}, f32[80,128]{1,0:T(8,128)S(1)}, u32[]{:S(2)}, u32[]{:S(2)}) collective-permute-start(f32[80,128]{1,0:T(8,128)S(1)} %get-tuple-element.20), channel_id=1, source_target_pairs={{0,6},{1,7},{2,0},{3,1},{4,2},{5,3},{6,4},{7,5},{8,14},{9,15},{10,... | collective-permute-start | bytes 122888 | tf_op jit(solution)/shard_map/ppermute | solution.py:52
  35.5 4.5 %collective-permute-start.7 = (f32[80,128]{1,0:T(8,128)S(1)}, f32[80,128]{1,0:T(8,128)S(1)}, u32[]{:S(2)}, u32[]{:S(2)}) collective-permute-start(f32[80,128]{1,0:T(8,128)S(1)} %get-tuple-element.20), channel_id=1, source_target_pairs={{0,2},{1,3},{2,4},{3,5},{4,6},{5,7},{6,0},{7,1},{8,10},{9,11},{10,... | collective-permute-start | bytes 122888 | tf_op jit(solution)/shard_map/ppermute | solution.py:52
  35.5 4.5 %collective-permute-start.6 = (f32[80,128]{1,0:T(8,128)S(1)}, f32[80,128]{1,0:T(8,128)S(1)}, u32[]{:S(2)}, u32[]{:S(2)}) collective-permute-start(f32[80,128]{1,0:T(8,128)S(1)} %get-tuple-element.20), channel_id=1, source_target_pairs={{0,4},{1,5},{2,6},{3,7},{4,0},{5,1},{6,2},{7,3},{8,12},{9,13},{10,... | collective-permute-start | bytes 122888 | tf_op jit(solution)/shard_map/ppermute | solution.py:52
  40.0 5.9 %collective-permute-start.9 = (f32[80,128]{1,0:T(8,128)S(1)}, f32[80,128]{1,0:T(8,128)S(1)}, u32[]{:S(2)}, u32[]{:S(2)}) collective-permute-start(f32[80,128]{1,0:T(8,128)S(1)} %add_add_fusion), channel_id=1, source_target_pairs={{0,1},{1,0},{2,3},{3,2},{4,5},{5,4},{6,7},{7,6},{8,9},{9,8},{10,11... | collective-permute-start | bytes 122888 | tf_op jit(solution)/shard_map/ppermute | solution.py:52
  45.9 3.1 %collective-permute-start.12 = (f32[80,128]{1,0:T(8,128)S(1)}, f32[80,128]{1,0:T(8,128)S(1)}, u32[]{:S(2)}, u32[]{:S(2)}) collective-permute-start(f32[80,128]{1,0:T(8,128)S(1)} %add.15), channel_id=1, source_target_pairs={{0,96},{1,25},{2,98},{3,27},{4,100},{5,29},{6,102},{7,31},{8,104},... | collective-permute-start | bytes 122888 | tf_op jit(solution)/shard_map/ppermute | solution.py:52
  47.8 4.4 %collective-permute-start.11 = (f32[80,128]{1,0:T(8,128)S(1)}, f32[80,128]{1,0:T(8,128)S(1)}, u32[]{:S(2)}, u32[]{:S(2)}) collective-permute-start(f32[80,128]{1,0:T(8,128)S(1)} %add.15), channel_id=1, source_target_pairs={{0,64},{1,17},{2,66},{3,19},{4,68},{5,21},{6,70},{7,23},{8,72},{9,... | collective-permute-start | bytes 122888 | tf_op jit(solution)/shard_map/ppermute | solution.py:52
  48.9 4.1 %collective-permute-start.10 = (f32[80,128]{1,0:T(8,128)S(1)}, f32[80,128]{1,0:T(8,128)S(1)}, u32[]{:S(2)}, u32[]{:S(2)}) collective-permute-start(f32[80,128]{1,0:T(8,128)S(1)} %add.15), channel_id=1, source_target_pairs={{0,32},{1,9},{2,34},{3,11},{4,36},{5,13},{6,38},{7,15},{8,40},{9,1... | collective-permute-start | bytes 122888 | tf_op jit(solution)/shard_map/ppermute | solution.py:52
  53.0 6.4 %collective-permute-start.15 = (f32[320,128]{1,0:T(8,128)S(1)}, f32[320,128]{1,0:T(8,128)S(1)}, u32[]{:S(2)}, u32[]{:S(2)}) collective-permute-start(f32[320,128]{1,0:T(8,128)S(1)} %pad_maximum_fusion.p0), channel_id=1, source_target_pairs={{0,24},{1,97},{2,26},{3,99},{4,28},{5,101},{6,30},{7,103},{8,0},{9... | collective-permute-start | bytes 491528 | tf_op jit(solution)/shard_map/ppermute | solution.py:52
  55.4 5.8 %collective-permute-start.14 = (f32[320,128]{1,0:T(8,128)S(1)}, f32[320,128]{1,0:T(8,128)S(1)}, u32[]{:S(2)}, u32[]{:S(2)}) collective-permute-start(f32[320,128]{1,0:T(8,128)S(1)} %pad_maximum_fusion.p0), channel_id=1, source_target_pairs={{0,16},{1,65},{2,18},{3,67},{4,20},{5,69},{6,22},{7,71},{8,24},{9,... | collective-permute-start | bytes 491528 | tf_op jit(solution)/shard_map/ppermute | solution.py:52
  55.4 7.4 %collective-permute-start.13 = (f32[320,128]{1,0:T(8,128)S(1)}, f32[320,128]{1,0:T(8,128)S(1)}, u32[]{:S(2)}, u32[]{:S(2)}) collective-permute-start(f32[320,128]{1,0:T(8,128)S(1)} %pad_maximum_fusion.p0), channel_id=1, source_target_pairs={{0,8},{1,33},{2,10},{3,35},{4,12},{5,37},{6,14},{7,39},{8,16},{9,4... | collective-permute-start | bytes 491528 | tf_op jit(solution)/shard_map/ppermute | solution.py:52

commit v3 on v2

--- a/solution.py
+++ b/solution.py
@@ -153,54 +153,55 @@
     )(freqs)
 
 
-def merge(refs, rows, weight, packed):
+def merge(refs, index, weight, packed, delta):
+    rows = 4 * PIECE
     wide = [
         jnp.concatenate([ref[rows + 32 * j : rows + 32 * (j + 1), :] for j in range(4)], axis=1) for ref in refs
     ]
     mean = ((wide[0] + wide[2]) + (wide[1] + wide[3])) * 0.25
-    delta = jnp.concatenate([part - mean for part in wide], axis=0)
+    for k, part in enumerate(wide):
+        delta[pl.ds(pl.multiple_of(GENS * ((index + 4 - k) % 4), GENS), GENS), :] = part - mean
     for i in range(4):
-        product = gram_of_few(delta, slice(BLOCK * i, BLOCK * (i + 1)))
+        product = gram_of_few(delta[...], slice(BLOCK * i, BLOCK * (i + 1)))
         for j in range(i, 4):
             n = PAIRS.index((i, j))
             packed[BLOCK * n : BLOCK * (n + 1), :] = product[:, BLOCK * (j - i) : BLOCK * (j - i + 1)] * weight
     return mean
 
 
-def first_kernel(*refs):
-    ins, outs, (packed, summed) = refs[:4], refs[4:8], refs[8:]
-    mean = merge(ins, 4 * PIECE, float(DEMES), packed)
-    first, second, core = place()
+def merged_rows(refs, first, core, packed, out):
     for j in range(4):
         rows = slice(PIECE * j, PIECE * (j + 1))
         row = pl.multiple_of(piece_row(core, first, j), 8)
-        summed[rows, :] = ((ins[0][rows, :] + ins[2][rows, :]) + (ins[1][rows, :] + ins[3][rows, :])) + packed[
+        out[rows, :] = ((refs[0][rows, :] + refs[2][rows, :]) + (refs[1][rows, :] + refs[3][rows, :])) + packed[
             pl.ds(row, PIECE), :
         ]
-    for k, out in enumerate(outs):
-        row = pl.multiple_of(PIECE * ((second + k) % 4), 8)
-        out[:PIECE, :] = summed[pl.ds(row, PIECE), :]
-        for j in range(4):
-            out[PIECE + 32 * j : PIECE + 32 * (j + 1), :] = mean[:, BLOCK * j : BLOCK * (j + 1)]
+
+
+def first_kernel(*refs):
+    ins, out, (packed, delta) = refs[:4], refs[4], refs[5:]
+    first, second, core = place()
+    mean = merge(ins, first, float(DEMES), packed, delta)
+    merged_rows(ins, first, core, packed, out)
+    for j in range(4):
+        out[4 * PIECE + 32 * j : 4 * PIECE + 32 * (j + 1), :] = mean[:, BLOCK * j : BLOCK * (j + 1)]
 
 
 def second_kernel(*refs):
-    ins, (out, mean_out), (packed,) = refs[:4], refs[4:6], refs[6:]
-    mean_out[...] = merge(ins, PIECE, 4.0 * DEMES, packed)
+    ins, (out, mean_out), (packed, delta) = refs[:4], refs[4:6], refs[6:]
     first, second, core = place()
-    row = pl.multiple_of(piece_row(core, first, second), 8)
-    rows = slice(0, PIECE)
-    out[...] = ((ins[0][rows, :] + ins[2][rows, :]) + (ins[1][rows, :] + ins[3][rows, :])) + packed[
-        pl.ds(row, PIECE), :
-    ]
+    mean_out[...] = merge(ins, second, 4.0 * DEMES, packed, delta)
+    merged_rows(ins, first, core, packed, out)
+
+
+MERGE_SCRATCH = [pltpu.VMEM((PACKED, BLOCK), jnp.float32), pltpu.VMEM((4 * GENS, LOCI), jnp.float32)]
 
 
 def merge_first(parts):
-    rows = PIECE + MEAN_ROWS
     return pl.pallas_call(
         first_kernel,
-        out_shape=[jax.ShapeDtypeStruct((rows, BLOCK), jnp.float32)] * 4,
-        scratch_shapes=[pltpu.VMEM((PACKED, BLOCK), jnp.float32), pltpu.VMEM((4 * PIECE, BLOCK), jnp.float32)],
+        out_shape=jax.ShapeDtypeStruct((4 * PIECE + MEAN_ROWS, BLOCK), jnp.float32),
+        scratch_shapes=MERGE_SCRATCH,
         compiler_params=pltpu.CompilerParams(vmem_limit_bytes=16 * MIB),
         name="merge_first",
     )(*parts)
@@ -210,10 +211,10 @@
     return pl.pallas_call(
         second_kernel,
         out_shape=[
-            jax.ShapeDtypeStruct((PIECE, BLOCK), jnp.float32),
+            jax.ShapeDtypeStruct((4 * PIECE, BLOCK), jnp.float32),
             jax.ShapeDtypeStruct((GENS, LOCI), jnp.float32),
         ],
-        scratch_shapes=[pltpu.VMEM((PACKED, BLOCK), jnp.float32)],
+        scratch_shapes=MERGE_SCRATCH,
         compiler_params=pltpu.CompilerParams(vmem_limit_bytes=16 * MIB),
         name="merge_second",
     )(*parts)
@@ -273,14 +274,29 @@
     return jnp.concatenate(rows, axis=0)
 
 
+def thirds(value):
+    one = value.astype(jnp.bfloat16)
+    value = value - one.astype(jnp.float32)
+    two = value.astype(jnp.bfloat16)
+    return one, two, (value - two.astype(jnp.float32)).astype(jnp.bfloat16)
+
+
+def plain(a, b):
+    return jnp.dot(a, b, preferred_element_type=jnp.float32)
+
+
+def rows_product(a, b):
+    return lax.dot_general(a, b, (((1,), (1,)), ((), ())), preferred_element_type=jnp.float32)
+
+
 STEP = 16
 STEPS = DEMES // STEP
 LOADS = 4
 
 
 def core_kernel(
-    p0, p1, p2, p3, start_ref, mean_ref, x_hbm, core_hbm, factor_ref,
-    x, core, packed, gram, both, hi_a, lo_a, hi_b, lo_b, loads, stores,
+    p0, p1, p2, p3, q0, q1, q2, q3, start_ref, mean_ref, x_hbm, core_hbm, factor_ref,
+    x, core, packed, gram, gram_1, gram_2, gram_3, both, hi_a, lo_a, hi_b, lo_b, loads, stores,
 ):
     def load(n):
         part = pl.ds(n * (DEMES // LOADS), DEMES // LOADS)
@@ -296,22 +312,40 @@
     first, second, core_id = place()
     for k, part in enumerate((p0, p1, p2, p3)):
         for l in range(4):
-            row = pl.multiple_of(piece_row(core_id, (first + 4 - k) % 4, (second + 4 - l) % 4), 8)
+            row = pl.multiple_of(piece_row(core_id, (first + 4 - k) % 4, l), 8)
             packed[pl.ds(row, PIECE), :] = part[PIECE * l : PIECE * (l + 1), :]
+    for k, part in enumerate((q0, q1, q2, q3)):
+        for l in range(4):
+            row = pl.multiple_of(piece_row(1 - core_id, (second + 4 - k) % 4, l), 8)
+            packed[pl.ds(row, PIECE), :] += part[PIECE * l : PIECE * (l + 1), :]
     for n, (i, j) in enumerate(PAIRS):
         block = packed[BLOCK * n : BLOCK * (n + 1), :] * (1.0 / (4096 * 256))
         gram[BLOCK * i : BLOCK * (i + 1), BLOCK * j : BLOCK * (j + 1)] = block
         if i != j:
             gram[BLOCK * j : BLOCK * (j + 1), BLOCK * i : BLOCK * (i + 1)] = block.T
 
+    gram_1[...], gram_2[...], gram_3[...] = thirds(gram[...])
+
     def body(_, basis):
-        z = jnp.dot(basis, gram[...], precision=lax.Precision.HIGHEST, preferred_element_type=jnp.float32)
-        small = lax.dot_general(
-            z, z, (((1,), (1,)), ((), ())), precision=lax.Precision.HIGHEST, preferred_element_type=jnp.float32
+        one, two, three = thirds(basis)
+        by_first = plain(jnp.concatenate([one, two, three], axis=0), gram_1[...])
+        by_second = plain(jnp.concatenate([one, two], axis=0), gram_2[...])
+        z = by_first[:RANK] + (
+            (by_first[RANK : 2 * RANK] + by_second[:RANK])
+            + ((by_first[2 * RANK :] + by_second[RANK:]) + plain(one, gram_3[...]))
         )
-        return jnp.dot(
-            inverse_cholesky(small), z, precision=lax.Precision.HIGHEST, preferred_element_type=jnp.float32
+        one, two, three = thirds(z)
+        wide = rows_product(jnp.concatenate([one, two, three], axis=0), jnp.concatenate([one, two], axis=0))
+        small = wide[:RANK, :RANK] + (
+            (wide[RANK : 2 * RANK, :RANK] + wide[:RANK, RANK:])
+            + ((wide[2 * RANK :, :RANK] + rows_product(one, three)) + wide[RANK : 2 * RANK, RANK:])
         )
+        w_one, w_two, w_three = thirds(inverse_cholesky(small))
+        w_pair = jnp.concatenate([w_one, w_two], axis=1)
+        large = plain(w_pair, jnp.concatenate([one, one], axis=0))
+        middle = plain(w_pair, jnp.concatenate([two, two], axis=0))
+        rest = plain(jnp.concatenate([w_one, w_three], axis=1), jnp.concatenate([three, one], axis=0))
+        return large + (middle + rest)
 
     basis = lax.fori_loop(0, ITERS, body, start_ref[...].T)
     factor = basis.T
@@ -342,7 +376,7 @@
         return carry
 
     split(0, hi_a, lo_a)
-    lax.fori_loop(0, STEPS // 2, pair, 0)
+    lax.fori_loop(0, STEPS // 2, pair, 0, unroll=2)
     for n in range(STEPS):
         store(n).wait()
 
@@ -352,7 +386,7 @@
     hbm = pl.BlockSpec(memory_space=pltpu.HBM)
     return pl.pallas_call(
         core_kernel,
-        in_specs=[vmem] * 6 + [hbm],
+        in_specs=[vmem] * 10 + [hbm],
         out_specs=[hbm, vmem],
         out_shape=[
             jax.ShapeDtypeStruct((DEMES, GENS, RANK), jnp.float32),
@@ -363,6 +397,9 @@
             pltpu.VMEM((DEMES, GENS, RANK), jnp.float32),
             pltpu.VMEM((PACKED, BLOCK), jnp.float32),
             pltpu.VMEM((LOCI, LOCI), jnp.float32),
+            pltpu.VMEM((LOCI, LOCI), jnp.bfloat16),
+            pltpu.VMEM((LOCI, LOCI), jnp.bfloat16),
+            pltpu.VMEM((LOCI, LOCI), jnp.bfloat16),
             pltpu.VMEM((LOCI, 2 * RANK), jnp.bfloat16),
         ]
         + [pltpu.VMEM((STEP * GENS, LOCI), jnp.bfloat16)] * 4
@@ -377,14 +414,13 @@
 
 def local(freqs, start_basis):
     out = local_gram(freqs)
-    parts = merge_first([out[0]] + [send(out[k], "first", k) for k in (1, 2, 3)])
-    shard, mean = merge_second([parts[0]] + [send(parts[k], "second", k) for k in (1, 2, 3)])
-    one, two, three = [send(shard, "x", k) for k in (1, 2, 3)]
-    shard = (shard + two) + (one + three)
-    shard = shard + send(shard, "core", 1)
-    row = jnp.concatenate([shard] + [send(shard, "second", k) for k in (1, 2, 3)], axis=0)
-    rows = [row] + [send(row, "first", k) for k in (1, 2, 3)]
-    return tuple(iterate(rows, start_basis, mean, freqs))
+    rows = merge_first([out[0]] + [send(out[k], "first", k) for k in (1, 2, 3)])
+    rows, mean = merge_second([rows] + [send(rows, "second", k) for k in (1, 2, 3)])
+    one, two, three = [send(rows, "x", k) for k in (1, 2, 3)]
+    rows = (rows + two) + (one + three)
+    parts = [rows] + [send(rows, "first", k) for k in (1, 2, 3)]
+    parts += [send(part, "core", 1) for part in parts]
+    return tuple(iterate(parts, start_basis, mean, freqs))
 
 
 def solution(mesh):

time: 91.2 us -> 88.3 us (0.968); the launches traced: 89.5 us -> 88.1 us
  starting transfers between devices: 26.7 us -> 29.9 us
  waiting for transfers between devices: 22.3 us -> 19.7 us
  Pallas kernels: 39.6 us -> 37.7 us
    ppermute x16, starting transfers between devices: 26.7 us -> 29.9 us  [send(): return lax.ppermute(value, AXES, shifted(kind, k))]
    ppermute x16, waiting for transfers between devices: 22.3 us -> 19.7 us  [send(): return lax.ppermute(value, AXES, shifted(kind, k))]
    pallas_call x3, Pallas kernels: 27.4 us -> 25.5 us  [the longest x1 24.6 us: iterate(): pl.pallas_call(core_kernel, in_specs=[vmem] * 10 + [hbm], out_specs=[hbm,...]
  transfers between devices with their start and end apart: 16 -> 16, of which waited for: 12 -> 8; matrix products, arithmetic and copies ran while one was open for 0% -> 0% of each run, Pallas kernels for 0% -> 0%
where the time goes in v3:
time: 88.3 us; the launch traced here: 88.1 us
  Pallas kernels  37.7 us (43%)
  starting transfers between devices  29.9 us (34%)
  waiting for transfers between devices  19.7 us (22%)
    ppermute x16, starting transfers between devices, send(): return lax.ppermute(value, AXES, shifted(kind, k))  29.9 us
    pallas_call x1, Pallas kernels, iterate(): pl.pallas_call(core_kernel, in_specs=[vmem] * 10 + [hbm], out_specs=[hbm,...  24.6 us
    ppermute x16, waiting for transfers between devices, send(): return lax.ppermute(value, AXES, shifted(kind, k))  19.7 us
    pallas_call x1, Pallas kernels, local_gram(): pl.pallas_call(gram_kernel, in_specs=[pl.BlockSpec(memory_space=pltpu.HBM...  12.2 us
  transfers between devices with their start and end apart: 16, of which 8 were waited for; matrix products, arithmetic and copies ran while one was open for 0% of the time, Pallas kernels for 0%

profile of v3, /device:TPU:1, one launch (start us, length us, event | category | flops | bytes accessed | tf_op | source)
XLA Modules:
  0.0 88.1 jit_solution(10120658914470284599)
XLA Ops:
  0.6 12.2 %local_gram.1 = (f32[448,128]{1,0:T(8,128)S(1)}, f32[448,128]{1,0:T(8,128)S(1)}, f32[448,128]{1,0:T(8,128)S(1)}, f32[448,128]{1,0:T(8,128)S(1)}) custom-call(f32[256,32,512]{2,1,0:T(8,128)} %x_hbm.3), custom_call_target="tpu_custom_call" | custom-call | tf_op jit(solution)/shard_map/local_gram/pallas_call | solution.py:136
  12.8 2.2 %collective-permute-start = (f32[448,128]{1,0:T(8,128)S(1)}, f32[448,128]{1,0:T(8,128)S(1)}, u32[]{:S(2)}, u32[]{:S(2)}) collective-permute-start(f32[448,128]{1,0:T(8,128)S(1)} %get-tuple-element.9), channel_id=1, source_target_pairs={{0,8},{1,33},{2,10},{3,35},{4,12},{5,37},{6,14},{7,39},{8,16},{9,4... | collective-permute-start | bytes 688136 | tf_op jit(solution)/shard_map/ppermute | solution.py:52
  15.0 2.6 %collective-permute-start.1 = (f32[448,128]{1,0:T(8,128)S(1)}, f32[448,128]{1,0:T(8,128)S(1)}, u32[]{:S(2)}, u32[]{:S(2)}) collective-permute-start(f32[448,128]{1,0:T(8,128)S(1)} %get-tuple-element.10), channel_id=1, source_target_pairs={{0,16},{1,65},{2,18},{3,67},{4,20},{5,69},{6,22},{7,71},{8,24},{9,... | collective-permute-start | bytes 688136 | tf_op jit(solution)/shard_map/ppermute | solution.py:52
  17.6 1.1 %collective-permute-start.2 = (f32[448,128]{1,0:T(8,128)S(1)}, f32[448,128]{1,0:T(8,128)S(1)}, u32[]{:S(2)}, u32[]{:S(2)}) collective-permute-start(f32[448,128]{1,0:T(8,128)S(1)} %get-tuple-element.11), channel_id=1, source_target_pairs={{0,24},{1,97},{2,26},{3,99},{4,28},{5,101},{6,30},{7,103},{8,0},{9... | collective-permute-start | bytes 688136 | tf_op jit(solution)/shard_map/ppermute | solution.py:52
  18.7 1.5 %collective-permute-done.refs_1_ = f32[448,128]{1,0:T(8,128)S(1)} collective-permute-done((f32[448,128]{1,0:T(8,128)S(1)}, f32[448,128]{1,0:T(8,128)S(1)}, u32[]{:S(2)}, u32[]{:S(2)}) %collective-permute-start) | collective-permute-done | bytes 229408 | tf_op jit(solution)/shard_map/ppermute | solution.py:52
  20.2 3.6 %collective-permute-done.1.refs_2_ = f32[448,128]{1,0:T(8,128)S(1)} collective-permute-done((f32[448,128]{1,0:T(8,128)S(1)}, f32[448,128]{1,0:T(8,128)S(1)}, u32[]{:S(2)}, u32[]{:S(2)}) %collective-permute-start.1) | collective-permute-done | bytes 229408 | tf_op jit(solution)/shard_map/ppermute | solution.py:52
  24.3 3.5 %collective-permute-start.5 = (f32[448,128]{1,0:T(8,128)S(1)}, f32[448,128]{1,0:T(8,128)S(1)}, u32[]{:S(2)}, u32[]{:S(2)}) collective-permute-start(f32[448,128]{1,0:T(8,128)S(1)} %merge_first.1.refs_0_), channel_id=1, source_target_pairs={{0,96},{1,25},{2,98},{3,27},{4,100},{5,29},{6,102},{7,31},{8,104},... | collective-permute-start | bytes 688136 | tf_op jit(solution)/shard_map/ppermute | solution.py:52
  27.8 0.7 collective-permute-start.3
  28.5 4.7 %collective-permute-done.5.refs_3_ = f32[448,128]{1,0:T(8,128)S(1)} collective-permute-done((f32[448,128]{1,0:T(8,128)S(1)}, f32[448,128]{1,0:T(8,128)S(1)}, u32[]{:S(2)}, u32[]{:S(2)}) %collective-permute-start.5) | collective-permute-done | bytes 229408 | tf_op jit(solution)/shard_map/ppermute | solution.py:52
  33.2 1.1 %collective-permute-done.4.refs_2_ = f32[448,128]{1,0:T(8,128)S(1)} collective-permute-done((f32[448,128]{1,0:T(8,128)S(1)}, f32[448,128]{1,0:T(8,128)S(1)}, u32[]{:S(2)}, u32[]{:S(2)}) %collective-permute-start.4) | collective-permute-done | bytes 229408 | tf_op jit(solution)/shard_map/ppermute | solution.py:52
  34.3 2.4 %collective-permute-done.3.refs_1_ = f32[448,128]{1,0:T(8,128)S(1)} collective-permute-done((f32[448,128]{1,0:T(8,128)S(1)}, f32[448,128]{1,0:T(8,128)S(1)}, u32[]{:S(2)}, u32[]{:S(2)}) %collective-permute-start.3) | collective-permute-done | bytes 229408 | tf_op jit(solution)/shard_map/ppermute | solution.py:52
  36.6 0.5 merge_second.1
  37.1 2.5 %collective-permute-start.8 = (f32[320,128]{1,0:T(8,128)S(1)}, f32[320,128]{1,0:T(8,128)S(1)}, u32[]{:S(2)}, u32[]{:S(2)}) collective-permute-start(f32[320,128]{1,0:T(8,128)S(1)} %get-tuple-element.12), channel_id=1, source_target_pairs={{0,6},{1,7},{2,0},{3,1},{4,2},{5,3},{6,4},{7,5},{8,14},{9,15},{10,... | collective-permute-start | bytes 491528 | tf_op jit(solution)/shard_map/ppermute | solution.py:52
  39.6 1.7 %collective-permute-start.6 = (f32[320,128]{1,0:T(8,128)S(1)}, f32[320,128]{1,0:T(8,128)S(1)}, u32[]{:S(2)}, u32[]{:S(2)}) collective-permute-start(f32[320,128]{1,0:T(8,128)S(1)} %get-tuple-element.12), channel_id=1, source_target_pairs={{0,4},{1,5},{2,6},{3,7},{4,0},{5,1},{6,2},{7,3},{8,12},{9,13},{10,... | collective-permute-start | bytes 491528 | tf_op jit(solution)/shard_map/ppermute | solution.py:52
  41.4 0.5 collective-permute-done.8
  41.9 4.9 %collective-permute-done.7 = f32[320,128]{1,0:T(8,128)S(1)} collective-permute-done((f32[320,128]{1,0:T(8,128)S(1)}, f32[320,128]{1,0:T(8,128)S(1)}, u32[]{:S(2)}, u32[]{:S(2)}) %collective-permute-start.7) | collective-permute-done | bytes 163872 | tf_op jit(solution)/shard_map/ppermute | solution.py:52
  46.8 3.0 %collective-permute-start.11 = (f32[320,128]{1,0:T(8,128)S(1)}, f32[320,128]{1,0:T(8,128)S(1)}, u32[]{:S(2)}, u32[]{:S(2)}) collective-permute-start(f32[320,128]{1,0:T(8,128)S(1)} %add_add_fusion.p0), channel_id=1, source_target_pairs={{0,24},{1,97},{2,26},{3,99},{4,28},{5,101},{6,30},{7,103},{8,0},{9... | collective-permute-start | bytes 491528 | tf_op jit(solution)/shard_map/ppermute | solution.py:52
  50.2 0.5 collective-permute-start.9
  50.8 4.8 %collective-permute-start.12 = (f32[320,128]{1,0:T(8,128)S(1)}, f32[320,128]{1,0:T(8,128)S(1)}, u32[]{:S(2)}, u32[]{:S(2)}) collective-permute-start(f32[320,128]{1,0:T(8,128)S(1)} %add_add_fusion.p0), channel_id=1, source_target_pairs={{0,1},{1,0},{2,3},{3,2},{4,5},{5,4},{6,7},{7,6},{8,9},{9,8},{10,11... | collective-permute-start | bytes 491528 | tf_op jit(solution)/shard_map/ppermute | solution.py:52
  55.5 2.9 %collective-permute-start.15 = (f32[320,128]{1,0:T(8,128)S(1)}, f32[320,128]{1,0:T(8,128)S(1)}, u32[]{:S(2)}, u32[]{:S(2)}) collective-permute-start(f32[320,128]{1,0:T(8,128)S(1)} %collective-permute-done.11.p3), channel_id=1, source_target_pairs={{0,1},{1,0},{2,3},{3,2},{4,5},{5,4},{6,7},{7,6},{8,9},{9,8},{10,11... | collective-permute-start | bytes 491528 | tf_op jit(solution)/shard_map/ppermute | solution.py:52
  58.4 2.3 %collective-permute-start.14 = (f32[320,128]{1,0:T(8,128)S(1)}, f32[320,128]{1,0:T(8,128)S(1)}, u32[]{:S(2)}, u32[]{:S(2)}) collective-permute-start(f32[320,128]{1,0:T(8,128)S(1)} %collective-permute-done.10.p2), channel_id=1, source_target_pairs={{0,1},{1,0},{2,3},{3,2},{4,5},{5,4},{6,7},{7,6},{8,9},{9,8},{10,11... | collective-permute-start | bytes 491528 | tf_op jit(solution)/shard_map/ppermute | solution.py:52
  60.6 1.7 %collective-permute-start.13 = (f32[320,128]{1,0:T(8,128)S(1)}, f32[320,128]{1,0:T(8,128)S(1)}, u32[]{:S(2)}, u32[]{:S(2)}) collective-permute-start(f32[320,128]{1,0:T(8,128)S(1)} %collective-permute-done.9.p1), channel_id=1, source_target_pairs={{0,1},{1,0},{2,3},{3,2},{4,5},{5,4},{6,7},{7,6},{8,9},{9,8},{10,11... | collective-permute-start | bytes 491528 | tf_op jit(solution)/shard_map/ppermute | solution.py:52
  62.3 1.0 %collective-permute-done.13.q1 = f32[320,128]{1,0:T(8,128)S(1)} collective-permute-done((f32[320,128]{1,0:T(8,128)S(1)}, f32[320,128]{1,0:T(8,128)S(1)}, u32[]{:S(2)}, u32[]{:S(2)}) %collective-permute-start.13) | collective-permute-done | bytes 163872 | tf_op jit(solution)/shard_map/ppermute | solution.py:52
  63.4 24.6 %iterate.1 = (f32[256,32,128]{2,1,0:T(8,128)}, f32[512,128]{1,0:T(8,128)}) custom-call(f32[320,128]{1,0:T(8,128)S(1)} %add_add_fusion.p0, f32[320,128]{1,0:T(8,128)S(1)} %collective-permute-done.9.p1, f32[320,128]{1,0:T(8,128)S(1)} %collective-permute-done.10.p2, f32[320,128]{1,0:T(8,128)S(1)} %collective-permute-done.11.p3, ...), custom_call_target="tpu_custom_call" | custom-call | tf_op jit(solution)/shard_map/iterate/pallas_call | solution.py:387
  (15 shorter events, 1.0 us)
Async XLA Ops:
  0.6 62.7 %copy-start = (f32[512,128]{1,0:T(8,128)S(1)}, f32[512,128]{1,0:T(8,128)}, u32[]{:S(2)}) copy-start(f32[512,128]{1,0:T(8,128)} %start_ref.1) | copy-start | bytes 786436
  12.8 7.3 %collective-permute-start = (f32[448,128]{1,0:T(8,128)S(1)}, f32[448,128]{1,0:T(8,128)S(1)}, u32[]{:S(2)}, u32[]{:S(2)}) collective-permute-start(f32[448,128]{1,0:T(8,128)S(1)} %get-tuple-element.9), channel_id=1, source_target_pairs={{0,8},{1,33},{2,10},{3,35},{4,12},{5,37},{6,14},{7,39},{8,16},{9,4... | collective-permute-start | bytes 688136 | tf_op jit(solution)/shard_map/ppermute | solution.py:52
  15.0 8.8 %collective-permute-start.1 = (f32[448,128]{1,0:T(8,128)S(1)}, f32[448,128]{1,0:T(8,128)S(1)}, u32[]{:S(2)}, u32[]{:S(2)}) collective-permute-start(f32[448,128]{1,0:T(8,128)S(1)} %get-tuple-element.10), channel_id=1, source_target_pairs={{0,16},{1,65},{2,18},{3,67},{4,20},{5,69},{6,22},{7,71},{8,24},{9,... | collective-permute-start | bytes 688136 | tf_op jit(solution)/shard_map/ppermute | solution.py:52
  17.6 6.2 %collective-permute-start.2 = (f32[448,128]{1,0:T(8,128)S(1)}, f32[448,128]{1,0:T(8,128)S(1)}, u32[]{:S(2)}, u32[]{:S(2)}) collective-permute-start(f32[448,128]{1,0:T(8,128)S(1)} %get-tuple-element.11), channel_id=1, source_target_pairs={{0,24},{1,97},{2,26},{3,99},{4,28},{5,101},{6,30},{7,103},{8,0},{9... | collective-permute-start | bytes 688136 | tf_op jit(solution)/shard_map/ppermute | solution.py:52
  24.3 9.0 %collective-permute-start.5 = (f32[448,128]{1,0:T(8,128)S(1)}, f32[448,128]{1,0:T(8,128)S(1)}, u32[]{:S(2)}, u32[]{:S(2)}) collective-permute-start(f32[448,128]{1,0:T(8,128)S(1)} %merge_first.1.refs_0_), channel_id=1, source_target_pairs={{0,96},{1,25},{2,98},{3,27},{4,100},{5,29},{6,102},{7,31},{8,104},... | collective-permute-start | bytes 688136 | tf_op jit(solution)/shard_map/ppermute | solution.py:52
  27.8 6.5 %collective-permute-start.4 = (f32[448,128]{1,0:T(8,128)S(1)}, f32[448,128]{1,0:T(8,128)S(1)}, u32[]{:S(2)}, u32[]{:S(2)}) collective-permute-start(f32[448,128]{1,0:T(8,128)S(1)} %merge_first.1.refs_0_), channel_id=1, source_target_pairs={{0,64},{1,17},{2,66},{3,19},{4,68},{5,21},{6,70},{7,23},{8,72},{9,... | collective-permute-start | bytes 688136 | tf_op jit(solution)/shard_map/ppermute | solution.py:52
  27.8 8.8 %collective-permute-start.3 = (f32[448,128]{1,0:T(8,128)S(1)}, f32[448,128]{1,0:T(8,128)S(1)}, u32[]{:S(2)}, u32[]{:S(2)}) collective-permute-start(f32[448,128]{1,0:T(8,128)S(1)} %merge_first.1.refs_0_), channel_id=1, source_target_pairs={{0,32},{1,9},{2,34},{3,11},{4,36},{5,13},{6,38},{7,15},{8,40},{9,1... | collective-permute-start | bytes 688136 | tf_op jit(solution)/shard_map/ppermute | solution.py:52
  37.1 4.8 %collective-permute-start.8 = (f32[320,128]{1,0:T(8,128)S(1)}, f32[320,128]{1,0:T(8,128)S(1)}, u32[]{:S(2)}, u32[]{:S(2)}) collective-permute-start(f32[320,128]{1,0:T(8,128)S(1)} %get-tuple-element.12), channel_id=1, source_target_pairs={{0,6},{1,7},{2,0},{3,1},{4,2},{5,3},{6,4},{7,5},{8,14},{9,15},{10,... | collective-permute-start | bytes 491528 | tf_op jit(solution)/shard_map/ppermute | solution.py:52
  39.6 7.1 %collective-permute-start.7 = (f32[320,128]{1,0:T(8,128)S(1)}, f32[320,128]{1,0:T(8,128)S(1)}, u32[]{:S(2)}, u32[]{:S(2)}) collective-permute-start(f32[320,128]{1,0:T(8,128)S(1)} %get-tuple-element.12), channel_id=1, source_target_pairs={{0,2},{1,3},{2,4},{3,5},{4,6},{5,7},{6,0},{7,1},{8,10},{9,11},{10,... | collective-permute-start | bytes 491528 | tf_op jit(solution)/shard_map/ppermute | solution.py:52
  39.6 7.1 %collective-permute-start.6 = (f32[320,128]{1,0:T(8,128)S(1)}, f32[320,128]{1,0:T(8,128)S(1)}, u32[]{:S(2)}, u32[]{:S(2)}) collective-permute-start(f32[320,128]{1,0:T(8,128)S(1)} %get-tuple-element.12), channel_id=1, source_target_pairs={{0,4},{1,5},{2,6},{3,7},{4,0},{5,1},{6,2},{7,3},{8,12},{9,13},{10,... | collective-permute-start | bytes 491528 | tf_op jit(solution)/shard_map/ppermute | solution.py:52
  46.8 8.7 %collective-permute-start.11 = (f32[320,128]{1,0:T(8,128)S(1)}, f32[320,128]{1,0:T(8,128)S(1)}, u32[]{:S(2)}, u32[]{:S(2)}) collective-permute-start(f32[320,128]{1,0:T(8,128)S(1)} %add_add_fusion.p0), channel_id=1, source_target_pairs={{0,24},{1,97},{2,26},{3,99},{4,28},{5,101},{6,30},{7,103},{8,0},{9... | collective-permute-start | bytes 491528 | tf_op jit(solution)/shard_map/ppermute | solution.py:52
  49.8 8.6 %collective-permute-start.10 = (f32[320,128]{1,0:T(8,128)S(1)}, f32[320,128]{1,0:T(8,128)S(1)}, u32[]{:S(2)}, u32[]{:S(2)}) collective-permute-start(f32[320,128]{1,0:T(8,128)S(1)} %add_add_fusion.p0), channel_id=1, source_target_pairs={{0,16},{1,65},{2,18},{3,67},{4,20},{5,69},{6,22},{7,71},{8,24},{9,... | collective-permute-start | bytes 491528 | tf_op jit(solution)/shard_map/ppermute | solution.py:52
  50.2 10.4 %collective-permute-start.9 = (f32[320,128]{1,0:T(8,128)S(1)}, f32[320,128]{1,0:T(8,128)S(1)}, u32[]{:S(2)}, u32[]{:S(2)}) collective-permute-start(f32[320,128]{1,0:T(8,128)S(1)} %add_add_fusion.p0), channel_id=1, source_target_pairs={{0,8},{1,33},{2,10},{3,35},{4,12},{5,37},{6,14},{7,39},{8,16},{9,4... | collective-permute-start | bytes 491528 | tf_op jit(solution)/shard_map/ppermute | solution.py:52
  50.8 11.6 %collective-permute-start.12 = (f32[320,128]{1,0:T(8,128)S(1)}, f32[320,128]{1,0:T(8,128)S(1)}, u32[]{:S(2)}, u32[]{:S(2)}) collective-permute-start(f32[320,128]{1,0:T(8,128)S(1)} %add_add_fusion.p0), channel_id=1, source_target_pairs={{0,1},{1,0},{2,3},{3,2},{4,5},{5,4},{6,7},{7,6},{8,9},{9,8},{10,11... | collective-permute-start | bytes 491528 | tf_op jit(solution)/shard_map/ppermute | solution.py:52
  55.5 6.8 %collective-permute-start.15 = (f32[320,128]{1,0:T(8,128)S(1)}, f32[320,128]{1,0:T(8,128)S(1)}, u32[]{:S(2)}, u32[]{:S(2)}) collective-permute-start(f32[320,128]{1,0:T(8,128)S(1)} %collective-permute-done.11.p3), channel_id=1, source_target_pairs={{0,1},{1,0},{2,3},{3,2},{4,5},{5,4},{6,7},{7,6},{8,9},{9,8},{10,11... | collective-permute-start | bytes 491528 | tf_op jit(solution)/shard_map/ppermute | solution.py:52
  58.4 4.0 %collective-permute-start.14 = (f32[320,128]{1,0:T(8,128)S(1)}, f32[320,128]{1,0:T(8,128)S(1)}, u32[]{:S(2)}, u32[]{:S(2)}) collective-permute-start(f32[320,128]{1,0:T(8,128)S(1)} %collective-permute-done.10.p2), channel_id=1, source_target_pairs={{0,1},{1,0},{2,3},{3,2},{4,5},{5,4},{6,7},{7,6},{8,9},{9,8},{10,11... | collective-permute-start | bytes 491528 | tf_op jit(solution)/shard_map/ppermute | solution.py:52
  60.6 2.7 %collective-permute-start.13 = (f32[320,128]{1,0:T(8,128)S(1)}, f32[320,128]{1,0:T(8,128)S(1)}, u32[]{:S(2)}, u32[]{:S(2)}) collective-permute-start(f32[320,128]{1,0:T(8,128)S(1)} %collective-permute-done.9.p1), channel_id=1, source_target_pairs={{0,1},{1,0},{2,3},{3,2},{4,5},{5,4},{6,7},{7,6},{8,9},{9,8},{10,11... | collective-permute-start | bytes 491528 | tf_op jit(solution)/shard_map/ppermute | solution.py:52

commit v4 on v3

--- a/solution.py
+++ b/solution.py
@@ -289,7 +289,7 @@
     return lax.dot_general(a, b, (((1,), (1,)), ((), ())), preferred_element_type=jnp.float32)
 
 
-STEP = 16
+STEP = 32
 STEPS = DEMES // STEP
 LOADS = 4
 
@@ -369,14 +369,14 @@
     def pair(p, carry):
         split(2 * p + 1, hi_b, lo_b)
         multiply(2 * p, hi_a, lo_a)
+        store(2 * p).start()
         split(jnp.minimum(2 * p + 2, STEPS - 1), hi_a, lo_a)
         multiply(2 * p + 1, hi_b, lo_b)
-        store(2 * p).start()
         store(2 * p + 1).start()
         return carry
 
     split(0, hi_a, lo_a)
-    lax.fori_loop(0, STEPS // 2, pair, 0, unroll=2)
+    lax.fori_loop(0, STEPS // 2, pair, 0)
     for n in range(STEPS):
         store(n).wait()
 

time: 88.3 us -> 88.3 us (level)
  no operation moved by 1% of the time
where the time goes in v4:
time: 88.3 us; the launch traced here: 88.2 us
  Pallas kernels  37.8 us (43%)
  starting transfers between devices  29.9 us (34%)
  waiting for transfers between devices  19.7 us (22%)
    ppermute x16, starting transfers between devices, send(): return lax.ppermute(value, AXES, shifted(kind, k))  29.9 us
    pallas_call x1, Pallas kernels, iterate(): pl.pallas_call(core_kernel, in_specs=[vmem] * 10 + [hbm], out_specs=[hbm,...  24.7 us
    ppermute x16, waiting for transfers between devices, send(): return lax.ppermute(value, AXES, shifted(kind, k))  19.7 us
    pallas_call x1, Pallas kernels, local_gram(): pl.pallas_call(gram_kernel, in_specs=[pl.BlockSpec(memory_space=pltpu.HBM...  12.2 us
  transfers between devices with their start and end apart: 16, of which 8 were waited for; matrix products, arithmetic and copies ran while one was open for 0% of the time, Pallas kernels for 0%

profile of v4, /device:TPU:1, one launch (start us, length us, event | category | flops | bytes accessed | tf_op | source)
XLA Modules:
  0.0 88.2 jit_solution(2609762117385549755)
XLA Ops:
  0.6 12.2 %local_gram.1 = (f32[448,128]{1,0:T(8,128)S(1)}, f32[448,128]{1,0:T(8,128)S(1)}, f32[448,128]{1,0:T(8,128)S(1)}, f32[448,128]{1,0:T(8,128)S(1)}) custom-call(f32[256,32,512]{2,1,0:T(8,128)} %x_hbm.3), custom_call_target="tpu_custom_call" | custom-call | tf_op jit(solution)/shard_map/local_gram/pallas_call | solution.py:136
  12.8 2.2 %collective-permute-start = (f32[448,128]{1,0:T(8,128)S(1)}, f32[448,128]{1,0:T(8,128)S(1)}, u32[]{:S(2)}, u32[]{:S(2)}) collective-permute-start(f32[448,128]{1,0:T(8,128)S(1)} %get-tuple-element.9), channel_id=1, source_target_pairs={{0,8},{1,33},{2,10},{3,35},{4,12},{5,37},{6,14},{7,39},{8,16},{9,4... | collective-permute-start | bytes 688136 | tf_op jit(solution)/shard_map/ppermute | solution.py:52
  15.0 2.6 %collective-permute-start.1 = (f32[448,128]{1,0:T(8,128)S(1)}, f32[448,128]{1,0:T(8,128)S(1)}, u32[]{:S(2)}, u32[]{:S(2)}) collective-permute-start(f32[448,128]{1,0:T(8,128)S(1)} %get-tuple-element.10), channel_id=1, source_target_pairs={{0,16},{1,65},{2,18},{3,67},{4,20},{5,69},{6,22},{7,71},{8,24},{9,... | collective-permute-start | bytes 688136 | tf_op jit(solution)/shard_map/ppermute | solution.py:52
  17.6 1.1 %collective-permute-start.2 = (f32[448,128]{1,0:T(8,128)S(1)}, f32[448,128]{1,0:T(8,128)S(1)}, u32[]{:S(2)}, u32[]{:S(2)}) collective-permute-start(f32[448,128]{1,0:T(8,128)S(1)} %get-tuple-element.11), channel_id=1, source_target_pairs={{0,24},{1,97},{2,26},{3,99},{4,28},{5,101},{6,30},{7,103},{8,0},{9... | collective-permute-start | bytes 688136 | tf_op jit(solution)/shard_map/ppermute | solution.py:52
  18.7 1.5 %collective-permute-done.refs_1_ = f32[448,128]{1,0:T(8,128)S(1)} collective-permute-done((f32[448,128]{1,0:T(8,128)S(1)}, f32[448,128]{1,0:T(8,128)S(1)}, u32[]{:S(2)}, u32[]{:S(2)}) %collective-permute-start) | collective-permute-done | bytes 229408 | tf_op jit(solution)/shard_map/ppermute | solution.py:52
  20.2 3.6 %collective-permute-done.1.refs_2_ = f32[448,128]{1,0:T(8,128)S(1)} collective-permute-done((f32[448,128]{1,0:T(8,128)S(1)}, f32[448,128]{1,0:T(8,128)S(1)}, u32[]{:S(2)}, u32[]{:S(2)}) %collective-permute-start.1) | collective-permute-done | bytes 229408 | tf_op jit(solution)/shard_map/ppermute | solution.py:52
  24.3 3.5 %collective-permute-start.5 = (f32[448,128]{1,0:T(8,128)S(1)}, f32[448,128]{1,0:T(8,128)S(1)}, u32[]{:S(2)}, u32[]{:S(2)}) collective-permute-start(f32[448,128]{1,0:T(8,128)S(1)} %merge_first.1.refs_0_), channel_id=1, source_target_pairs={{0,96},{1,25},{2,98},{3,27},{4,100},{5,29},{6,102},{7,31},{8,104},... | collective-permute-start | bytes 688136 | tf_op jit(solution)/shard_map/ppermute | solution.py:52
  27.8 0.7 collective-permute-start.3
  28.5 4.7 %collective-permute-done.5.refs_3_ = f32[448,128]{1,0:T(8,128)S(1)} collective-permute-done((f32[448,128]{1,0:T(8,128)S(1)}, f32[448,128]{1,0:T(8,128)S(1)}, u32[]{:S(2)}, u32[]{:S(2)}) %collective-permute-start.5) | collective-permute-done | bytes 229408 | tf_op jit(solution)/shard_map/ppermute | solution.py:52
  33.2 1.1 %collective-permute-done.4.refs_2_ = f32[448,128]{1,0:T(8,128)S(1)} collective-permute-done((f32[448,128]{1,0:T(8,128)S(1)}, f32[448,128]{1,0:T(8,128)S(1)}, u32[]{:S(2)}, u32[]{:S(2)}) %collective-permute-start.4) | collective-permute-done | bytes 229408 | tf_op jit(solution)/shard_map/ppermute | solution.py:52
  34.3 2.4 %collective-permute-done.3.refs_1_ = f32[448,128]{1,0:T(8,128)S(1)} collective-permute-done((f32[448,128]{1,0:T(8,128)S(1)}, f32[448,128]{1,0:T(8,128)S(1)}, u32[]{:S(2)}, u32[]{:S(2)}) %collective-permute-start.3) | collective-permute-done | bytes 229408 | tf_op jit(solution)/shard_map/ppermute | solution.py:52
  36.6 0.5 merge_second.1
  37.1 2.5 %collective-permute-start.8 = (f32[320,128]{1,0:T(8,128)S(1)}, f32[320,128]{1,0:T(8,128)S(1)}, u32[]{:S(2)}, u32[]{:S(2)}) collective-permute-start(f32[320,128]{1,0:T(8,128)S(1)} %get-tuple-element.12), channel_id=1, source_target_pairs={{0,6},{1,7},{2,0},{3,1},{4,2},{5,3},{6,4},{7,5},{8,14},{9,15},{10,... | collective-permute-start | bytes 491528 | tf_op jit(solution)/shard_map/ppermute | solution.py:52
  39.6 1.7 %collective-permute-start.6 = (f32[320,128]{1,0:T(8,128)S(1)}, f32[320,128]{1,0:T(8,128)S(1)}, u32[]{:S(2)}, u32[]{:S(2)}) collective-permute-start(f32[320,128]{1,0:T(8,128)S(1)} %get-tuple-element.12), channel_id=1, source_target_pairs={{0,4},{1,5},{2,6},{3,7},{4,0},{5,1},{6,2},{7,3},{8,12},{9,13},{10,... | collective-permute-start | bytes 491528 | tf_op jit(solution)/shard_map/ppermute | solution.py:52
  41.4 0.5 collective-permute-done.8
  41.9 4.9 %collective-permute-done.7 = f32[320,128]{1,0:T(8,128)S(1)} collective-permute-done((f32[320,128]{1,0:T(8,128)S(1)}, f32[320,128]{1,0:T(8,128)S(1)}, u32[]{:S(2)}, u32[]{:S(2)}) %collective-permute-start.7) | collective-permute-done | bytes 163872 | tf_op jit(solution)/shard_map/ppermute | solution.py:52
  46.8 3.0 %collective-permute-start.11 = (f32[320,128]{1,0:T(8,128)S(1)}, f32[320,128]{1,0:T(8,128)S(1)}, u32[]{:S(2)}, u32[]{:S(2)}) collective-permute-start(f32[320,128]{1,0:T(8,128)S(1)} %add_add_fusion.p0), channel_id=1, source_target_pairs={{0,24},{1,97},{2,26},{3,99},{4,28},{5,101},{6,30},{7,103},{8,0},{9... | collective-permute-start | bytes 491528 | tf_op jit(solution)/shard_map/ppermute | solution.py:52
  50.2 0.5 collective-permute-start.9
  50.8 4.8 %collective-permute-start.12 = (f32[320,128]{1,0:T(8,128)S(1)}, f32[320,128]{1,0:T(8,128)S(1)}, u32[]{:S(2)}, u32[]{:S(2)}) collective-permute-start(f32[320,128]{1,0:T(8,128)S(1)} %add_add_fusion.p0), channel_id=1, source_target_pairs={{0,1},{1,0},{2,3},{3,2},{4,5},{5,4},{6,7},{7,6},{8,9},{9,8},{10,11... | collective-permute-start | bytes 491528 | tf_op jit(solution)/shard_map/ppermute | solution.py:52
  55.5 2.9 %collective-permute-start.15 = (f32[320,128]{1,0:T(8,128)S(1)}, f32[320,128]{1,0:T(8,128)S(1)}, u32[]{:S(2)}, u32[]{:S(2)}) collective-permute-start(f32[320,128]{1,0:T(8,128)S(1)} %collective-permute-done.11.p3), channel_id=1, source_target_pairs={{0,1},{1,0},{2,3},{3,2},{4,5},{5,4},{6,7},{7,6},{8,9},{9,8},{10,11... | collective-permute-start | bytes 491528 | tf_op jit(solution)/shard_map/ppermute | solution.py:52
  58.4 2.3 %collective-permute-start.14 = (f32[320,128]{1,0:T(8,128)S(1)}, f32[320,128]{1,0:T(8,128)S(1)}, u32[]{:S(2)}, u32[]{:S(2)}) collective-permute-start(f32[320,128]{1,0:T(8,128)S(1)} %collective-permute-done.10.p2), channel_id=1, source_target_pairs={{0,1},{1,0},{2,3},{3,2},{4,5},{5,4},{6,7},{7,6},{8,9},{9,8},{10,11... | collective-permute-start | bytes 491528 | tf_op jit(solution)/shard_map/ppermute | solution.py:52
  60.6 1.7 %collective-permute-start.13 = (f32[320,128]{1,0:T(8,128)S(1)}, f32[320,128]{1,0:T(8,128)S(1)}, u32[]{:S(2)}, u32[]{:S(2)}) collective-permute-start(f32[320,128]{1,0:T(8,128)S(1)} %collective-permute-done.9.p1), channel_id=1, source_target_pairs={{0,1},{1,0},{2,3},{3,2},{4,5},{5,4},{6,7},{7,6},{8,9},{9,8},{10,11... | collective-permute-start | bytes 491528 | tf_op jit(solution)/shard_map/ppermute | solution.py:52
  62.3 1.0 %collective-permute-done.13.q1 = f32[320,128]{1,0:T(8,128)S(1)} collective-permute-done((f32[320,128]{1,0:T(8,128)S(1)}, f32[320,128]{1,0:T(8,128)S(1)}, u32[]{:S(2)}, u32[]{:S(2)}) %collective-permute-start.13) | collective-permute-done | bytes 163872 | tf_op jit(solution)/shard_map/ppermute | solution.py:52
  63.4 24.7 %iterate.1 = (f32[256,32,128]{2,1,0:T(8,128)}, f32[512,128]{1,0:T(8,128)}) custom-call(f32[320,128]{1,0:T(8,128)S(1)} %add_add_fusion.p0, f32[320,128]{1,0:T(8,128)S(1)} %collective-permute-done.9.p1, f32[320,128]{1,0:T(8,128)S(1)} %collective-permute-done.10.p2, f32[320,128]{1,0:T(8,128)S(1)} %collective-permute-done.11.p3, ...), custom_call_target="tpu_custom_call" | custom-call | tf_op jit(solution)/shard_map/iterate/pallas_call | solution.py:387
  (15 shorter events, 1.0 us)
Async XLA Ops:
  0.6 62.7 %copy-start = (f32[512,128]{1,0:T(8,128)S(1)}, f32[512,128]{1,0:T(8,128)}, u32[]{:S(2)}) copy-start(f32[512,128]{1,0:T(8,128)} %start_ref.1) | copy-start | bytes 786436
  12.8 7.3 %collective-permute-start = (f32[448,128]{1,0:T(8,128)S(1)}, f32[448,128]{1,0:T(8,128)S(1)}, u32[]{:S(2)}, u32[]{:S(2)}) collective-permute-start(f32[448,128]{1,0:T(8,128)S(1)} %get-tuple-element.9), channel_id=1, source_target_pairs={{0,8},{1,33},{2,10},{3,35},{4,12},{5,37},{6,14},{7,39},{8,16},{9,4... | collective-permute-start | bytes 688136 | tf_op jit(solution)/shard_map/ppermute | solution.py:52
  15.0 8.8 %collective-permute-start.1 = (f32[448,128]{1,0:T(8,128)S(1)}, f32[448,128]{1,0:T(8,128)S(1)}, u32[]{:S(2)}, u32[]{:S(2)}) collective-permute-start(f32[448,128]{1,0:T(8,128)S(1)} %get-tuple-element.10), channel_id=1, source_target_pairs={{0,16},{1,65},{2,18},{3,67},{4,20},{5,69},{6,22},{7,71},{8,24},{9,... | collective-permute-start | bytes 688136 | tf_op jit(solution)/shard_map/ppermute | solution.py:52
  17.6 6.2 %collective-permute-start.2 = (f32[448,128]{1,0:T(8,128)S(1)}, f32[448,128]{1,0:T(8,128)S(1)}, u32[]{:S(2)}, u32[]{:S(2)}) collective-permute-start(f32[448,128]{1,0:T(8,128)S(1)} %get-tuple-element.11), channel_id=1, source_target_pairs={{0,24},{1,97},{2,26},{3,99},{4,28},{5,101},{6,30},{7,103},{8,0},{9... | collective-permute-start | bytes 688136 | tf_op jit(solution)/shard_map/ppermute | solution.py:52
  24.3 9.0 %collective-permute-start.5 = (f32[448,128]{1,0:T(8,128)S(1)}, f32[448,128]{1,0:T(8,128)S(1)}, u32[]{:S(2)}, u32[]{:S(2)}) collective-permute-start(f32[448,128]{1,0:T(8,128)S(1)} %merge_first.1.refs_0_), channel_id=1, source_target_pairs={{0,96},{1,25},{2,98},{3,27},{4,100},{5,29},{6,102},{7,31},{8,104},... | collective-permute-start | bytes 688136 | tf_op jit(solution)/shard_map/ppermute | solution.py:52
  27.8 6.5 %collective-permute-start.4 = (f32[448,128]{1,0:T(8,128)S(1)}, f32[448,128]{1,0:T(8,128)S(1)}, u32[]{:S(2)}, u32[]{:S(2)}) collective-permute-start(f32[448,128]{1,0:T(8,128)S(1)} %merge_first.1.refs_0_), channel_id=1, source_target_pairs={{0,64},{1,17},{2,66},{3,19},{4,68},{5,21},{6,70},{7,23},{8,72},{9,... | collective-permute-start | bytes 688136 | tf_op jit(solution)/shard_map/ppermute | solution.py:52
  27.8 8.8 %collective-permute-start.3 = (f32[448,128]{1,0:T(8,128)S(1)}, f32[448,128]{1,0:T(8,128)S(1)}, u32[]{:S(2)}, u32[]{:S(2)}) collective-permute-start(f32[448,128]{1,0:T(8,128)S(1)} %merge_first.1.refs_0_), channel_id=1, source_target_pairs={{0,32},{1,9},{2,34},{3,11},{4,36},{5,13},{6,38},{7,15},{8,40},{9,1... | collective-permute-start | bytes 688136 | tf_op jit(solution)/shard_map/ppermute | solution.py:52
  37.1 4.8 %collective-permute-start.8 = (f32[320,128]{1,0:T(8,128)S(1)}, f32[320,128]{1,0:T(8,128)S(1)}, u32[]{:S(2)}, u32[]{:S(2)}) collective-permute-start(f32[320,128]{1,0:T(8,128)S(1)} %get-tuple-element.12), channel_id=1, source_target_pairs={{0,6},{1,7},{2,0},{3,1},{4,2},{5,3},{6,4},{7,5},{8,14},{9,15},{10,... | collective-permute-start | bytes 491528 | tf_op jit(solution)/shard_map/ppermute | solution.py:52
  39.6 7.1 %collective-permute-start.7 = (f32[320,128]{1,0:T(8,128)S(1)}, f32[320,128]{1,0:T(8,128)S(1)}, u32[]{:S(2)}, u32[]{:S(2)}) collective-permute-start(f32[320,128]{1,0:T(8,128)S(1)} %get-tuple-element.12), channel_id=1, source_target_pairs={{0,2},{1,3},{2,4},{3,5},{4,6},{5,7},{6,0},{7,1},{8,10},{9,11},{10,... | collective-permute-start | bytes 491528 | tf_op jit(solution)/shard_map/ppermute | solution.py:52
  39.6 7.1 %collective-permute-start.6 = (f32[320,128]{1,0:T(8,128)S(1)}, f32[320,128]{1,0:T(8,128)S(1)}, u32[]{:S(2)}, u32[]{:S(2)}) collective-permute-start(f32[320,128]{1,0:T(8,128)S(1)} %get-tuple-element.12), channel_id=1, source_target_pairs={{0,4},{1,5},{2,6},{3,7},{4,0},{5,1},{6,2},{7,3},{8,12},{9,13},{10,... | collective-permute-start | bytes 491528 | tf_op jit(solution)/shard_map/ppermute | solution.py:52
  46.8 8.7 %collective-permute-start.11 = (f32[320,128]{1,0:T(8,128)S(1)}, f32[320,128]{1,0:T(8,128)S(1)}, u32[]{:S(2)}, u32[]{:S(2)}) collective-permute-start(f32[320,128]{1,0:T(8,128)S(1)} %add_add_fusion.p0), channel_id=1, source_target_pairs={{0,24},{1,97},{2,26},{3,99},{4,28},{5,101},{6,30},{7,103},{8,0},{9... | collective-permute-start | bytes 491528 | tf_op jit(solution)/shard_map/ppermute | solution.py:52
  49.8 8.6 %collective-permute-start.10 = (f32[320,128]{1,0:T(8,128)S(1)}, f32[320,128]{1,0:T(8,128)S(1)}, u32[]{:S(2)}, u32[]{:S(2)}) collective-permute-start(f32[320,128]{1,0:T(8,128)S(1)} %add_add_fusion.p0), channel_id=1, source_target_pairs={{0,16},{1,65},{2,18},{3,67},{4,20},{5,69},{6,22},{7,71},{8,24},{9,... | collective-permute-start | bytes 491528 | tf_op jit(solution)/shard_map/ppermute | solution.py:52
  50.2 10.4 %collective-permute-start.9 = (f32[320,128]{1,0:T(8,128)S(1)}, f32[320,128]{1,0:T(8,128)S(1)}, u32[]{:S(2)}, u32[]{:S(2)}) collective-permute-start(f32[320,128]{1,0:T(8,128)S(1)} %add_add_fusion.p0), channel_id=1, source_target_pairs={{0,8},{1,33},{2,10},{3,35},{4,12},{5,37},{6,14},{7,39},{8,16},{9,4... | collective-permute-start | bytes 491528 | tf_op jit(solution)/shard_map/ppermute | solution.py:52
  50.8 11.6 %collective-permute-start.12 = (f32[320,128]{1,0:T(8,128)S(1)}, f32[320,128]{1,0:T(8,128)S(1)}, u32[]{:S(2)}, u32[]{:S(2)}) collective-permute-start(f32[320,128]{1,0:T(8,128)S(1)} %add_add_fusion.p0), channel_id=1, source_target_pairs={{0,1},{1,0},{2,3},{3,2},{4,5},{5,4},{6,7},{7,6},{8,9},{9,8},{10,11... | collective-permute-start | bytes 491528 | tf_op jit(solution)/shard_map/ppermute | solution.py:52
  55.5 6.8 %collective-permute-start.15 = (f32[320,128]{1,0:T(8,128)S(1)}, f32[320,128]{1,0:T(8,128)S(1)}, u32[]{:S(2)}, u32[]{:S(2)}) collective-permute-start(f32[320,128]{1,0:T(8,128)S(1)} %collective-permute-done.11.p3), channel_id=1, source_target_pairs={{0,1},{1,0},{2,3},{3,2},{4,5},{5,4},{6,7},{7,6},{8,9},{9,8},{10,11... | collective-permute-start | bytes 491528 | tf_op jit(solution)/shard_map/ppermute | solution.py:52
  58.4 4.0 %collective-permute-start.14 = (f32[320,128]{1,0:T(8,128)S(1)}, f32[320,128]{1,0:T(8,128)S(1)}, u32[]{:S(2)}, u32[]{:S(2)}) collective-permute-start(f32[320,128]{1,0:T(8,128)S(1)} %collective-permute-done.10.p2), channel_id=1, source_target_pairs={{0,1},{1,0},{2,3},{3,2},{4,5},{5,4},{6,7},{7,6},{8,9},{9,8},{10,11... | collective-permute-start | bytes 491528 | tf_op jit(solution)/shard_map/ppermute | solution.py:52
  60.6 2.7 %collective-permute-start.13 = (f32[320,128]{1,0:T(8,128)S(1)}, f32[320,128]{1,0:T(8,128)S(1)}, u32[]{:S(2)}, u32[]{:S(2)}) collective-permute-start(f32[320,128]{1,0:T(8,128)S(1)} %collective-permute-done.9.p1), channel_id=1, source_target_pairs={{0,1},{1,0},{2,3},{3,2},{4,5},{5,4},{6,7},{7,6},{8,9},{9,8},{10,11... | collective-permute-start | bytes 491528 | tf_op jit(solution)/shard_map/ppermute | solution.py:52
